TPU v7x, 32 devices: a whole 2x2x4 slice. The times are simulated.
32 devices in a mesh: fsdp: 2 (over x), ctx: 4 (over z), tp: 4 (over y, core).
Axes of the slice: x: 2, y: 2, z: 4, core: 2. Of those that a mesh axis runs over, the one named last changes fastest.
Arguments:
- inputs: bfloat16 [4, 2048, 1024], P('fsdp', 'ctx'), may hold values from -6 to 6
- cotangent: bfloat16 [4, 2048, 1024], P('fsdp', 'ctx'), may hold values from -6 to 6
- lengths: int32 [4], P('fsdp'), may hold values from 256 to 2048, as said below
- attention_gain: bfloat16 [1024], P('fsdp'), may hold values from 0.099609375 to 1.8984375
- triple_weight: bfloat16 [1024, 3, 1024], P('fsdp', None, 'tp'), may hold values from -0.1875 to 0.1875
- mixing_weight: bfloat16 [1024, 1024], P('tp', 'fsdp'), may hold values from -6 to 6
- feedforward_gain: bfloat16 [1024], P('fsdp'), may hold values from 0.099609375 to 1.8984375
- lifting_weight: bfloat16 [1024, 2, 2624], P('fsdp', None, 'tp'), may hold values from -0.1875 to 0.1875
- down_weight: bfloat16 [2624, 1024], P('tp', 'fsdp'), may hold values from -0.125 to 0.125
Outputs:
- output: bfloat16 [4, 2048, 1024], P('fsdp', 'ctx')
- input_gradient: bfloat16 [4, 2048, 1024], P('fsdp', 'ctx')
- attention_gain_gradient: float32 [1024], P('fsdp')
- triple_gradient: float32 [1024, 3, 1024], P('fsdp', None, 'tp')
- mixing_gradient: float32 [1024, 1024], P('tp', 'fsdp')
- feedforward_gain_gradient: float32 [1024], P('fsdp')
- lifting_gradient: float32 [1024, 2, 2624], P('fsdp', None, 'tp')
- down_gradient: float32 [2624, 1024], P('tp', 'fsdp')
Inputs may be any that keep to these rules, and one draw needn't show every extreme that they name: `lengths`: in each aligned group of 2 sequences, one drawn at random has length 2048.
All inputs are finite; a program needn't handle non-finite values.
Results may differ from a plain program's by a relative error of at most 0.022.
Values may be sent and summed in bfloat16 or wider, within the bound.
No kernel may reach another device: no remote copies, remote signals or barrier semaphores. Data moves between devices by JAX's collectives and lax.ppermute only.
A program may use at most 192 MiB of HBM per device.

v0:
```python
import functools

import jax
import jax.numpy as jnp
from jax import lax
from jax.experimental import pallas as pl
from jax.experimental.pallas import tpu as pltpu
from jax.sharding import PartitionSpec as P

H = 16
NORM_EPS = 1e-05
ROPE_BASE = 160000.0
MASKED = -1e30
LOG2E = 1.4426950408889634
BF = jnp.bfloat16
F32 = jnp.float32
FLOPS_PER_US = 1153e6
SCALE = 0.764
WEIGHTS = {"attend_back": 25.94, "attention_grad": 16.5, "feed": 3.975, "feed_grad1": 2.168, "gradient_join": 4.874, "halve": 6.466, "mix": 2.703, "norm_first_back": 0.02256, "output_join": 0.2996, "pieces": 0.09989, "project_back": 4.301, "project_sum": 0.2843, "sum_ctx": 4.169}
WAIT_KEYS, WAIT_REST, WAIT_MIXING = (1,), (1,), True
FETCH = {"keys": "mixing", "first": "feed"}
ORDER = (
    "SB0 PC0 SB1 EX",
    "AB0 FG1 PC1 FG2",
    "I1 AB1 BR I2",
    "PB0 O1 PS0 PB1",
    "FB0 AT PS1 OT",
    "I3 O2 FB1 I4",
    "A1 O3 OO A2",
    "O4 JG A3 A4",
    "OJ",
)
CORE, ROW = 1, 2


def nn(a, b):
    return lax.dot_general(a, b, (((1,), (0,)), ((), ())), preferred_element_type=F32)


def nt(a, b):
    return lax.dot_general(a, b, (((1,), (1,)), ((), ())), preferred_element_type=F32)


def tn(a, b):
    return lax.dot_general(a, b, (((0,), (0,)), ((), ())), preferred_element_type=F32)


def swap(array, axis, size, step):
    return lax.ppermute(array, axis, [(i, i ^ step) for i in range(size)])


def part(start, size):
    return pl.ds(pl.multiple_of(start * size, size), size)


def piece(refs, z, m):
    return refs[m] if len(refs) == 4 else refs[0].at[z ^ m]


class Part:
    def __init__(self, array, index):
        self.array, self.index = array, index


class Sequence:
    def __init__(self):
        self.last = None

    def __call__(self, body, scalars, arrays, outs, scratch=(), us=1, name=None, wait=(), mib=16):
        operands = [a.array if isinstance(a, Part) else a for a in arrays]
        specs = [pl.BlockSpec(memory_space=pltpu.VMEM)] * len(arrays)
        after = list(wait) + ([] if self.last is None else [self.last])
        first = len(scalars) + len(arrays)

        def run(*refs):
            taken = refs[len(scalars) : first]
            taken = [
                r.at[a.index] if isinstance(a, Part) else r
                for r, a in zip(taken, arrays, strict=True)
            ]
            body(*refs[: len(scalars)], *taken, *refs[first + len(after) :])

        results = pl.pallas_call(
            run,
            out_shape=[jax.ShapeDtypeStruct(s, t) for s, t in outs],
            in_specs=[pl.BlockSpec(memory_space=pltpu.SMEM)] * len(scalars)
            + specs
            + [pl.BlockSpec(memory_space=pl.ANY)] * len(after),
            out_specs=[pl.BlockSpec(memory_space=pltpu.VMEM)] * len(outs),
            scratch_shapes=list(scratch),
            compiler_params=pltpu.CompilerParams(vmem_limit_bytes=mib << 20),
            cost_estimate=pl.CostEstimate(
                flops=int(WEIGHTS.get(name, us) * SCALE * FLOPS_PER_US), bytes_accessed=0, transcendentals=0
            ),
            name=name,
        )(*scalars, *operands, *after)
        self.last = min(results, key=lambda r: r.size)
        return results


def whole_gain(gain, xi):
    own, other = gain[0:1, :].astype(F32), gain[1:2, :].astype(F32)
    low = jnp.where(xi == 0, own, other)
    high = jnp.where(xi == 0, other, own)
    return jnp.concatenate([low, high], axis=1)


def norm_body(place, x, gain, out):
    gain_row = whole_gain(gain, place[2])
    step = 256
    for s in range(x.shape[0]):

        def block(i, carry, s=s):
            at = part(i, step)
            v = x[s, at, :].astype(F32)
            center = v - jnp.mean(v, axis=-1, keepdims=True)
            spread = jnp.mean(center * center, axis=-1, keepdims=True)
            out[s, at, :] = (center * lax.rsqrt(spread + NORM_EPS) * gain_row).astype(BF)
            return carry

        lax.fori_loop(0, x.shape[1] // step, block, 0)


def project_body(size, kinds, place, *refs):
    normed, cosine, sine = refs[0:3]
    weights = refs[3 : 3 + 2 * len(kinds)]
    outs, heads = refs[3 + 2 * len(kinds) : -1], refs[-1]
    count = len(outs)
    half = weights[0].shape[0]
    z, xi = place[0], place[2]
    blocks = normed.shape[0] if len(normed.shape) == 3 else 1
    span = normed.shape[-2]
    for s in range(blocks):
        rows = slice(s * span, (s + 1) * span)
        source = normed.at[s] if len(normed.shape) == 3 else normed
        n_own = source[:, part(xi, half)]
        n_other = source[:, part(1 - xi, half)]
        for i, rotated in enumerate(kinds):
            acc = nt(weights[2 * i][...].T, n_own) + nt(weights[2 * i + 1][...].T, n_other)
            for h in range(count):
                u = acc[h * size : (h + 1) * size]
                if rotated:
                    u1, u2 = u[: size // 2], u[size // 2 :]
                    co, si = cosine[...], sine[...]
                    u = jnp.concatenate([u1 * co - u2 * si, u2 * co + u1 * si], axis=0)
                heads[h, i * size : (i + 1) * size, rows] = u.astype(BF)
    for m in range(count):
        outs[m][...] = heads[z ^ m]


def attend_body(s, span, place, lengths, *refs):
    k, qv = refs[0:4], refs[4:8]
    *o, o_full, lse, keys, values, top, total = refs[8:]
    z = place[0]
    size = k[0].shape[0]
    cols = slice(s * span, (s + 1) * span)
    values[:, size:, :] = jnp.ones((4, values.shape[1] - size, span), BF)
    for m in range(4):
        keys[z ^ m] = k[m][:, cols].T
        values[z ^ m, :size, :] = qv[m][size:, :]
    top[...] = jnp.full_like(top, MASKED)
    total[...] = jnp.zeros_like(total)
    length = lengths[s]
    full = length // span
    rest = length - full * span
    unit = size**-0.5 * LOG2E

    def step(j, limit):
        key, value = keys[j], values[j]
        for m in range(4):
            raw = nn(key, qv[m][:size, :])
            if limit is not None:
                raw = jnp.where(lax.broadcasted_iota(jnp.int32, raw.shape, 0) < limit, raw, MASKED)
            before = top[m : m + 1, :]
            peak = jnp.maximum(before, jnp.max(raw, axis=0, keepdims=True))
            p = jnp.exp2((raw - peak) * unit)
            top[m : m + 1, :] = peak
            total[m] = total[m] * jnp.exp2((before - peak) * unit) + nn(value, p.astype(BF))

    def whole(j, carry):
        step(j, None)
        return carry

    lax.fori_loop(0, full, whole, 0)

    @pl.when(rest > 0)
    def _():
        step(full, rest)

    for m in range(4):
        normaliser = total[m, size : size + 1, :]
        result = total[m, :size, :] / normaliser
        o_full[m] = result
        piece(o, z, m)[...] = result.astype(BF)
        lse[m : m + 1, :] = top[m : m + 1, :] * unit + jnp.log(normaliser) * LOG2E


def attend_back_body(s, span, place, lengths, *refs):
    k, qv = refs[0:4], refs[4:8]
    keys, keys_t, values, d_query, d_key, d_value, queries, grads, delta = refs[-9:]
    count = (len(refs) - 21) // 2
    do, out = refs[8 : 8 + count], refs[12 + count : -9]
    o_full, lse, cosine, sine = refs[8 + count : 12 + count]
    z = place[0]
    size = k[0].shape[0]
    cols = slice(s * span, (s + 1) * span)
    for m in range(4):
        keys[z ^ m] = k[m][:, cols].T
        keys_t[z ^ m] = k[m][:, cols]
        values[z ^ m] = qv[m][size:, :].T
        queries[m] = qv[m][:size, :].T
        grads[m] = piece(do, z, m)[...].T
        delta[m : m + 1, :] = jnp.sum(piece(do, z, m)[...].astype(F32) * o_full[m], axis=0, keepdims=True)
    d_query[...] = jnp.zeros_like(d_query)
    d_key[...] = jnp.zeros_like(d_key)
    d_value[...] = jnp.zeros_like(d_value)
    length = lengths[s]
    full = length // span
    rest = length - full * span
    factor = size**-0.5

    def step(j, limit):
        key, key_t, value = keys[j], keys_t[j], values[j]
        for m in range(4):
            raw = nn(key, qv[m][:size, :])
            if limit is not None:
                raw = jnp.where(lax.broadcasted_iota(jnp.int32, raw.shape, 0) < limit, raw, MASKED)
            p = jnp.exp2(raw * (factor * LOG2E) - lse[m : m + 1, :])
            dp = nn(value, piece(do, z, m)[...])
            ds = (p * (dp - delta[m : m + 1, :])).astype(BF)
            d_value[j] += nn(p.astype(BF), grads[m])
            d_key[j] += nn(ds, queries[m])
            d_query[m] += nn(key_t, ds)

    def whole(j, carry):
        step(j, None)
        return carry

    lax.fori_loop(0, full, whole, 0)

    @pl.when(rest > 0)
    def _():
        step(full, rest)

    def back(w, j):
        at = part(j, span)
        co, si = cosine[:, at], sine[:, at]
        w1, w2 = w[: size // 2] * factor, w[size // 2 :] * factor
        return jnp.concatenate([w1 * co + w2 * si, w2 * co - w1 * si], axis=0).astype(BF)

    for m in range(4):
        j = z ^ m
        target = piece(out, z, m)
        target[0:size, :] = back(d_query[m], j)
        target[size : 2 * size, :] = back(d_key[j].T, j)
        target[2 * size :, :] = d_value[j].T.astype(BF)


def heads_body(place, *refs):
    *o, mixed = refs
    size = mixed.shape[0] // 4
    for m in range(4):
        mixed[part(place[0] ^ m, size), :] = piece(o, place[0], m)[...]


def mix_body(place, mixed, *refs):
    *weights, out = refs
    c, xi = place[1], place[2]
    width, half = weights[0].shape
    rows = out.shape[0]
    left = [mixed[part(at, width), part(c, rows)].T for at in (c, 1 - c)]
    for side, hi in ((0, xi), (1, 1 - xi)):
        total = nn(left[0], weights[side][...]) + nn(left[1], weights[2 + side][...])
        out[:, part(hi, half)] = total.astype(BF)


def add_body(a, b, out):
    out[...] = (a[...].astype(F32) + b[...].astype(F32)).astype(out.dtype)


def feed_body(place, mine, theirs, x, gain, cot, *refs):
    weights = refs[0:4]
    middle, out, out_grad, *packs = refs[4:]
    c, xi = place[1], place[2]
    rows, width = middle.shape
    half = width // 2
    units = weights[0].shape[0] // 3
    lanes = (packs[0].shape[1] - width) // 3
    token_rows = part(c, rows)
    v = x[token_rows, :].astype(F32) + (mine[...].astype(F32) + theirs[...].astype(F32))
    middle[...] = v
    center = v - jnp.mean(v, axis=-1, keepdims=True)
    spread = jnp.mean(center * center, axis=-1, keepdims=True)
    n = (center * lax.rsqrt(spread + NORM_EPS) * whole_gain(gain, place[2])).astype(BF)
    columns = (part(xi, half), part(1 - xi, half))
    packs[0][:, :width] = n
    packs[1][:, :width] = n
    totals, totals_grad = [None, None], [None, None]
    for i, pack in enumerate(packs):
        sides = weights[2 * i : 2 * i + 2]

        def over(left, rows_of, sides=sides):
            return sum(nt(left(cols), w[rows_of, :]) for w, cols in zip(sides, columns))

        inner, gate, down = (slice(k * units, (k + 1) * units) for k in range(3))
        a = over(lambda cols, pack=pack: pack[:, cols], inner)
        b = over(lambda cols, pack=pack: pack[:, cols], gate)
        dh = over(lambda cols: cot[token_rows, cols], down)
        cdf = 0.5 * (1.0 + lax.erf(a * (0.5**0.5)))
        act = a * cdf
        slope = cdf + a * jnp.exp(-0.5 * a * a) * (0.5 * 2.0**0.5 / jnp.pi**0.5)
        h = (act * b).astype(BF)
        da = (dh * b * slope).astype(BF)
        db = (dh * act).astype(BF)
        for k, value in enumerate((h, da, db)):
            pack[:, width + k * lanes : width + k * lanes + units] = value
        for side, w in enumerate(sides):
            term = nn(da, w[inner, :]) + nn(db, w[gate, :])
            totals_grad[side] = term if i == 0 else totals_grad[side] + term
            term = nn(h, w[down, :])
            totals[side] = term if i == 0 else totals[side] + term
    for side, cols in enumerate(columns):
        out_grad[:, cols] = totals_grad[side].astype(BF)
        out[:, cols] = totals[side].astype(BF)


def feed_grad_body(units, kinds, place, *refs):
    *packs, cot, keep, send = refs
    c, xi = place[1], place[2]
    half = keep.shape[1]
    rows, lanes = packs[0].shape
    lanes = (lanes - 2 * half) // 3
    for target, hi in ((send, 1 - xi), (keep, xi)):
        for row, kind in enumerate(kinds):
            total = None
            for i, pack in enumerate(packs):
                start = 2 * half + kind * lanes
                if kind == 0:
                    right = cot[i // 2, part(c if i % 2 == 0 else 1 - c, rows), part(hi, half)]
                else:
                    right = pack[:, part(hi, half)]
                term = tn(pack[:, start : start + units], right)
                total = term if total is None else total + term
            target[row * units : (row + 1) * units, :] = total.astype(target.dtype)


def attention_grad_body(place, *refs):
    stacks, (normed,), gains, mixed, branches = refs[0:2], refs[2:3], refs[3:7], refs[7:9], refs[9:13]
    keep, send = refs[13:]
    c, xi = place[1], place[2]
    half = keep.shape[1]
    rows = stacks[0].shape[0]
    width = rows // 3
    under = keep.shape[0] - rows - width
    tokens = branches[0].shape[0]
    for target, hi in ((send, 1 - xi), (keep, xi)):
        cols = part(hi, half)
        total = nn(stacks[0][...], normed[0, :, cols]) + nn(stacks[1][...], normed[1, :, cols])
        target[0:rows, :] = total.astype(target.dtype)
        first = gains[0][:, cols] + gains[1][:, cols]
        second = 0.5 * (gains[2][:, cols] + gains[3][:, cols])
        which = lax.broadcasted_iota(jnp.int32, (under, half), 0)
        both = jnp.where(which == 0, first, jnp.where(which == 1, second, 0.0))
        target[rows : rows + under, :] = both.astype(target.dtype)
        total = None
        for s in range(2):
            for side, at in ((0, c), (1, 1 - c)):
                left = mixed[s][part(c, width), part(at, tokens)]
                term = nn(left, branches[2 * s + side][:, cols])
                total = term if total is None else total + term
        target[rows + under :, :] = total.astype(target.dtype)


def halve_body(which, place, a, b, keep, send):
    columns = keep.shape[1]
    for target, at in ((send, 1 - place[which]), (keep, place[which])):
        cols = part(at, columns)
        total = a[:, cols].astype(F32) + b[:, cols].astype(F32)
        target[...] = total.astype(target.dtype)


def unite_body(which, place, mine, theirs, out):
    columns = mine.shape[1]
    out[:, part(place[which], columns)] = mine[...].astype(out.dtype)
    out[:, part(1 - place[which], columns)] = theirs[...].astype(out.dtype)


def feed_end_body(which, place, mine0, theirs0, mine1, theirs1, lifting, down):
    columns = mine0.shape[1]
    units = down.shape[0]
    for first, second, at in ((mine0, mine1, place[which]), (theirs0, theirs1, 1 - place[which])):
        cols = part(at, columns)
        lifting[0, :, cols] = first[...].astype(F32)
        lifting[1, :, cols] = second[0:units, :].astype(F32)
        down[:, cols] = second[units:, :].astype(F32)


def attention_end_body(which, place, mine, theirs, triple, mixing, gains):
    columns = mine.shape[1]
    width = triple.shape[2]
    for part_of, at in ((mine, place[which]), (theirs, 1 - place[which])):
        cols = part(at, columns)
        for kind in range(3):
            value = part_of[kind * width : (kind + 1) * width, :]
            triple[kind, cols, :] = value.T.astype(F32)
        gains[:, cols] = part_of[3 * width : 3 * width + 16, :].astype(F32)[0:2]
        mixing[:, cols] = part_of[part_of.shape[0] - width :, :].astype(F32)


def norm_back(v, gain, grad):
    center = v - jnp.mean(v, axis=-1, keepdims=True)
    spread = jnp.mean(center * center, axis=-1, keepdims=True)
    r = lax.rsqrt(spread + NORM_EPS)
    xhat = center * r
    eg = grad * gain
    mean_eg = jnp.mean(eg, axis=-1, keepdims=True)
    mean_egx = jnp.mean(eg * xhat, axis=-1, keepdims=True)
    back = r * (eg - mean_eg - xhat * mean_egx)
    return back, jnp.sum(grad * xhat, axis=0, keepdims=True)


def second_back_body(place, mine, theirs, middle, cot, gain, *refs):
    *weights, middle_grad, branch, gain_grad, product = refs
    c, xi = place[1], place[2]
    rows = middle.shape[0]
    heads_width, half = weights[0].shape
    grad = mine[...].astype(F32) + theirs[...].astype(F32)
    back, total = norm_back(middle[...], whole_gain(gain, xi), grad)
    result = cot[part(c, rows), :].astype(F32) + back
    middle_grad[...] = result
    branch[...] = result.astype(BF)
    gain_grad[...] = total
    left, right = branch[:, part(xi, half)], branch[:, part(1 - xi, half)]
    for i, at in ((0, c), (1, 1 - c)):
        term = nt(weights[2 * i][...], left) + nt(weights[2 * i + 1][...], right)
        product[part(at, heads_width), :] = term.astype(BF)


def pieces_body(place, product, *outs):
    z, c = place[0], place[1]
    rows, columns = product.shape
    size = rows // 16
    for m in range(4):
        for k in range(2):
            rows_here = part(8 * k + 4 * c + (z ^ m), size)
            piece(outs, z, m)[:, k * columns : (k + 1) * columns] = product[rows_here, :]


def first_back_body(place, mine, theirs, x, middle_grad, gain, out):
    rows = middle_grad.shape[0]
    grad = mine[...].astype(F32) + theirs[...].astype(F32)
    back, _ = norm_back(x[part(place[1], rows), :].astype(F32), whole_gain(gain, place[2]), grad)
    out[...] = (middle_grad[...] + back).astype(BF)


def output_body(place, m0, m1, f0, f1, theirs, out):
    for s, (m, f) in enumerate(((m0, f0), (m1, f1))):
        out[s] = (m[...] + (f[...].astype(F32) + theirs[s].astype(F32))).astype(BF)


def join_body(place, *refs):
    *parts, out = refs
    rows = parts[0].shape[0]
    for s in range(len(parts) // 2):
        out[s, part(place[1], rows), :] = parts[2 * s][...]
        out[s, part(1 - place[1], rows), :] = parts[2 * s + 1][...]


def join_stacked_body(place, own, other, out):
    rows = own.shape[1]
    out[:, part(place[1], rows), :] = own[...]
    out[:, part(1 - place[1], rows), :] = other[...]


def project_back_body(place, *refs):
    *d, x = refs[:-10]
    weights, (keep, send, stacked, gain_grad) = refs[-10:-4], refs[-4:]
    c, rows = place[1], keep.shape[0]
    z, xi = place[0], place[2]
    half, width = weights[0].shape
    size = d[0].shape[-2] // 3
    for m in range(4):
        here = piece(d, z, m)
        for kind in range(3):
            at = part(kind * (width // size) + (z ^ m), size)
            stacked[at, :] = here[kind * size : (kind + 1) * size, :]
    for target, at in ((send, 1 - c), (keep, c)):
        tokens = stacked[:, part(at, rows)].T
        v = x[part(at, rows), :].astype(F32)
        mean = jnp.mean(v, axis=-1, keepdims=True)
        center = v - mean
        r = lax.rsqrt(jnp.mean(center * center, axis=-1, keepdims=True) + NORM_EPS)
        for side, hi in ((0, xi), (1, 1 - xi)):
            total = None
            for kind in range(3):
                term = nt(
                    tokens[:, kind * width : (kind + 1) * width], weights[2 * kind + side][...]
                )
                total = term if total is None else total + term
            cols = part(hi, half)
            target[:, cols] = total.astype(target.dtype)
            xhat = (x[part(at, rows), cols].astype(F32) - mean) * r
            sums = jnp.sum(total * xhat, axis=0, keepdims=True)
            if target is send:
                gain_grad[:, cols] = sums
            else:
                gain_grad[:, cols] += sums


def on_device(
    inputs,
    cotangent,
    lengths,
    attention_gain,
    triple_weight,
    mixing_weight,
    feedforward_gain,
    lifting_weight,
    down_weight,
    sizes,
):
    run = Sequence()
    pairs = sizes["fsdp"] == 2
    sequences, span, width = inputs.shape
    half = width // 2
    heads_width = triple_weight.shape[2]
    size = width // H
    heads = heads_width // size
    units = down_weight.shape[0]
    z = lax.axis_index("ctx")
    core = lax.axis_index("tp") % 2
    xi = lax.axis_index("fsdp") if pairs else jnp.int32(0)
    place = jnp.stack([z, core, xi, z % 2, z // 2]).astype(jnp.int32)
    quarter = span // 2
    both = range(sequences)

    def gather(array, axis):
        if pairs:
            return array, swap(array, "fsdp", 2, 1)
        full = lax.all_gather(array, "fsdp", axis=axis, tiled=True)
        return lax.split(full, [full.shape[axis] // 2] * 2, axis=axis)

    def over_fsdp(keep, send):
        if pairs:
            return keep, swap(send, "fsdp", 2, 1)
        full = jnp.concatenate([keep.astype(BF), send], axis=1)
        keep = lax.psum_scatter(full, "fsdp", scatter_dimension=1, tiled=True)
        return keep, jnp.zeros_like(keep)

    def added(a, b, kind, name):
        return run(add_body, [], [a, b], [(b.shape, kind)], name=name)[0]

    cores = [[0, 1], [2, 3]]

    def both_cores(array):
        return lax.all_gather(array, "tp", axis_index_groups=cores, axis=0, tiled=True)

    def redistribute(pieces):
        moved = {m: swap(pieces[m], "ctx", 4, m) for m in (2, 3, 1)}
        return [pieces[0], moved[1], moved[2], moved[3]]

    low, high = 3, 4

    class Reduction:
        def __init__(self, keep, send):
            self.a, self.b = over_fsdp(keep, send)
            if not pairs:
                self.a = lax.psum(self.a, "ctx").astype(F32)

        def halve(self, which, step):
            if not pairs:
                return
            rows, columns = self.a.shape
            shape = (rows, columns // 2)
            self.a, send = run(
                functools.partial(halve_body, which),
                [place],
                [self.a, self.b],
                [(shape, F32), (shape, BF)],
                us=1,
                name="halve",
            )
            self.b = swap(send, "ctx", 4, step)

        def unite(self, which, kind):
            if not pairs:
                return
            rows, columns = self.b.shape
            shape = (rows, columns * 2)
            (self.a,) = run(
                functools.partial(unite_body, which),
                [place],
                [self.a, self.b],
                [(shape, kind)],
                us=0.7,
                name="unite",
            )

        def first(self):
            self.halve(low, 1)

        def second(self):
            self.halve(high, 2)

        def third(self):
            if not pairs:
                return
            (self.a,) = run(
                add_body, [], [self.a, self.b], [(self.b.shape, BF)], us=0.4, name="sum_ctx"
            )
            self.b = swap(self.a, "ctx", 4, 2)

        def fourth(self):
            if not pairs:
                return
            self.unite(high, BF)
            self.b = swap(self.a, "ctx", 4, 1)

    key_w = gather(triple_weight[:, 1], 0)
    gains_own, gains_other = gather(jnp.stack([attention_gain, feedforward_gain]), 1)
    first_gain = jnp.stack([gains_own[0], gains_other[0]])
    second_gain = jnp.stack([gains_own[1], gains_other[1]])

    full_length = span * sizes["ctx"]
    frequency = ROPE_BASE ** (-2.0 * jnp.arange(size // 2, dtype=F32) / size)
    angles = frequency[:, None] * jnp.arange(full_length, dtype=jnp.int32).astype(F32)[None, :]
    cosine, sine = jnp.cos(angles), jnp.sin(angles)
    cosine_here = lax.dynamic_slice_in_dim(cosine, z * span, span, 1)
    sine_here = lax.dynamic_slice_in_dim(sine, z * span, span, 1)

    (normed_first,) = run(
        norm_body, [place], [inputs, first_gain], [(inputs.shape, BF)], name="norm_first"
    )

    def later(array):
        return lax.optimization_barrier((array, run.last))[0]

    query_w = gather(later(triple_weight[:, 0]), 0)
    value_w = gather(later(triple_weight[:, 2]), 0)

    def project(normed, kinds, weights, columns, wait=()):
        return redistribute(
            run(
                functools.partial(project_body, size, kinds),
                [place],
                [normed, cosine_here, sine_here, *weights],
                [((len(kinds) * size, columns), BF)] * heads,
                scratch=[pltpu.VMEM((heads, len(kinds) * size, columns), BF)],
                us=1.3,
                wait=wait,
                name="project",
            )
        )

    keys = project(normed_first, (True,), key_w, sequences * span)
    first, second = Part(normed_first, 0), Part(normed_first, 1)
    feed_own = jnp.concatenate(
        [lifting_weight[:, 0].T, lifting_weight[:, 1].T, down_weight], axis=0
    )
    fetched = {}

    def fetch(point):
        for name in FETCH.get(point, "").split():
            source = {"mixing": mixing_weight, "feed": feed_own}[name]
            fetched[name] = gather(later(source), 1)

    fetch("keys")
    rest = [project(first, (True, False), (*query_w, *value_w), span, [keys[i] for i in WAIT_KEYS])]
    fetch("first")
    waits = [keys[i] for i in (1, 2, 3) if i not in WAIT_KEYS]
    waits += [rest[0][i] for i in WAIT_REST]
    waits += [fetched["mixing"][1]] if WAIT_MIXING and "mixing" in fetched else []
    rest.append(project(second, (True, False), (*query_w, *value_w), span, waits))
    fetch("second")

    attended = []

    def attend(s, wait):
        *o, o_full, lse = run(
            functools.partial(attend_body, s, span),
            [place, lengths],
            [*keys, *rest[s]],
            [*[((size, span), BF)] * 4, ((4, size, span), F32), ((4, span), F32)],
            scratch=[
                pltpu.VMEM((4, span, size), BF),
                pltpu.VMEM((4, size + 16, span), BF),
                pltpu.VMEM((4, span), F32),
                pltpu.VMEM((4, size + 16, span), F32),
            ],
            us=10,
            wait=wait,
            name="attend",
        )
        attended.append((redistribute(o), o_full, lse))

    attend(0, [])
    fetch("attend")
    mixing_w, feed_w = fetched["mixing"], fetched["feed"]
    attend(1, [])

    mixtures, sums, mixing_all = [], [], list(mixing_w)

    def mix(s, wait):
        (mixed,) = run(
            heads_body,
            [place],
            attended[s][0],
            [((heads_width, span), BF)],
            us=0.6,
            wait=wait,
            name="heads",
        )
        if s == 0:
            mixing_all.extend(swap(later(w), "tp", 4, CORE) for w in mixing_w)
        mixed = both_cores(mixed)
        mixtures.append(mixed)
        (mine,) = run(
            mix_body, [place], [mixed, *mixing_all], [((quarter, width), BF)], us=1, name="mix"
        )
        sums.append((mine, swap(mine, "tp", 4, ROW)))

    mix(0, [])
    feed_theirs = [swap(later(w), "tp", 4, CORE) for w in feed_w]
    mix(1, [])

    feeds, grads, packs = [], [], []
    lanes = -(-units // 128) * 128
    for s in both:
        feed = run(
            feed_body,
            [place],
            [*sums[s], Part(inputs, s), second_gain, Part(cotangent, s), *feed_w, *feed_theirs],
            [
                ((quarter, width), F32),
                ((quarter, width), BF),
                ((quarter, width), BF),
                ((quarter, width + 3 * lanes), BF),
                ((quarter, width + 3 * lanes), BF),
            ],
            us=6.6,
            name="feed",
        )
        feeds.append(feed)
        grads.append((feed[2], swap(feed[2], "tp", 4, ROW)))
        packs.append((feed[3], feed[4]))
    rows = 3 * heads_width
    branches, middle_grads, gain_second, mixture_grads = {}, {}, {}, {}
    products, exchanged, reductions, d, partials = {}, [], {}, {}, {}
    stacks, gain_first, back_sums, inputs_own, made = {}, {}, {}, {}, {}

    def second_back(s):
        middle_grads[s], branches[s], gain_second[s], products[s] = run(
            second_back_body,
            [place],
            [*grads[s], feeds[s][0], Part(cotangent, s), second_gain, *mixing_all],
            [
                ((quarter, width), F32),
                ((quarter, width), BF),
                ((1, width), F32),
                ((2 * heads_width, quarter), BF),
            ],
            us=2,
            name="norm_second_back",
        )

    def pieces(s):
        cut = run(
            pieces_body,
            [place],
            [both_cores(products[s])],
            [((size, span), BF)] * 4,
            us=0.6,
            name="pieces",
        )
        mixture_grads[s] = redistribute(cut)

    def exchange_packs():
        for mine, theirs in packs:
            exchanged.extend([mine, swap(later(theirs), "tp", 4, CORE)])

    def feed_grad(key, kinds):
        count = len(kinds) * units
        reductions[key] = Reduction(
            *run(
                functools.partial(feed_grad_body, units, kinds),
                [place],
                [*exchanged, cotangent],
                [((count, half), F32), ((count, half), BF)],
                us=1.7 * len(kinds),
                name="feed_grad" + str(len(kinds)),
            )
        )

    def attend_back(s):
        _, o_full, lse = attended[s]
        d[s] = redistribute(
            run(
                functools.partial(attend_back_body, s, span),
                [place, lengths],
                [*keys, *rest[s], *mixture_grads[s], o_full, lse, cosine, sine],
                [((3 * size, span), BF)] * 4,
                scratch=[
                    pltpu.VMEM((4, span, size), BF),
                    pltpu.VMEM((4, size, span), BF),
                    pltpu.VMEM((4, span, size), BF),
                    pltpu.VMEM((4, size, span), F32),
                    pltpu.VMEM((4, span, size), F32),
                    pltpu.VMEM((4, span, size), F32),
                    pltpu.VMEM((4, span, size), BF),
                    pltpu.VMEM((4, span, size), BF),
                    pltpu.VMEM((4, span), F32),
                ],
                us=13,
                name="attend_back",
            )
        )

    def project_back(s):
        keep, send, stacks[s], gain_first[s] = run(
            project_back_body,
            [place],
            [*d[s], Part(inputs, s), *query_w, *key_w, *value_w],
            [
                ((quarter, width), F32),
                ((quarter, width), BF),
                ((3 * heads_width, span), BF),
                ((1, width), F32),
            ],
            us=2.4,
            name="project_back",
        )
        partials[s] = (keep, swap(send, "tp", 4, CORE))

    def project_sum(s):
        (mine,) = run(
            add_body, [], partials[s], [((quarter, width), BF)], us=0.4, name="project_sum"
        )
        back_sums[s] = (mine, swap(mine, "tp", 4, ROW))

    def first_back(s):
        (own,) = run(
            first_back_body,
            [place],
            [*back_sums[s], Part(inputs, s), middle_grads[s], first_gain],
            [((quarter, width), BF)],
            us=1.3,
            name="norm_first_back",
        )
        inputs_own[s] = (own, swap(own, "tp", 4, CORE))

    def exchange_branches():
        made["branches"] = [
            b for s in both for b in (branches[s], swap(later(branches[s]), "tp", 4, CORE))
        ]

    def attention_grad():
        sums = [gain_first[0], gain_first[1], gain_second[0], gain_second[1]]
        reductions["A"] = Reduction(
            *run(
                attention_grad_body,
                [place],
                [stacks[0], stacks[1], normed_first, *sums, *mixtures, *made["branches"]],
                [
                    ((rows + 16 + heads_width, half), F32),
                    ((rows + 16 + heads_width, half), BF),
                ],
                us=4.5,
                name="attention_grad",
            )
        )

    def output_start():
        made["out"] = swap(later(jnp.stack([f[1] for f in feeds])), "tp", 4, ROW)

    def output_own():
        (own,) = run(
            output_body,
            [place],
            [*[f[0] for f in feeds], *[f[1] for f in feeds], made["out"]],
            [((sequences, quarter, width), BF)],
            name="output",
        )
        made["out"] = (own, swap(own, "tp", 4, CORE))

    def output_join():
        (made["output"],) = run(
            join_stacked_body, [place], made["out"], [(inputs.shape, BF)], name="output_join"
        )

    def gradient_join():
        (made["gradient"],) = run(
            join_body,
            [place],
            [*inputs_own[0], *inputs_own[1]],
            [(inputs.shape, BF)],
            name="gradient_join",
        )

    steps = {
        "EX": exchange_packs,
        "FG1": lambda: feed_grad("I", (1,)),
        "FG2": lambda: feed_grad("O", (2, 0)),
        "BR": exchange_branches,
        "AT": attention_grad,
        "OT": output_start,
        "OO": output_own,
        "OJ": output_join,
        "JG": gradient_join,
    }
    for s in both:
        steps["SB" + str(s)] = functools.partial(second_back, s)
        steps["PC" + str(s)] = functools.partial(pieces, s)
        steps["AB" + str(s)] = functools.partial(attend_back, s)
        steps["PB" + str(s)] = functools.partial(project_back, s)
        steps["PS" + str(s)] = functools.partial(project_sum, s)
        steps["FB" + str(s)] = functools.partial(first_back, s)
    for line in ORDER:
        for step in line.split():
            if step in steps:
                steps[step]()
            else:
                stage = ("first", "second", "third", "fourth")[int(step[1]) - 1]
                getattr(reductions[step[0]], stage)()
    inner_grad, other_grad, attention_grad = (reductions[k] for k in "IOA")
    output, input_gradient = made["output"], made["gradient"]
    if pairs:
        lifting_gradient, down_gradient = run(
            functools.partial(feed_end_body, low),
            [place],
            [inner_grad.a, inner_grad.b, other_grad.a, other_grad.b],
            [((2, units, half), F32), ((units, half), F32)],
            us=2.5,
            name="feed_end",
        )
        triple_gradient, mixing_gradient, gain_parts = run(
            functools.partial(attention_end_body, low),
            [place],
            [attention_grad.a, attention_grad.b],
            [((3, half, heads_width), F32), ((heads_width, half), F32), ((2, half), F32)],
            us=2,
            name="attention_end",
        )
    else:
        lifting_gradient = jnp.stack([inner_grad.a, other_grad.a[:units]])
        down_gradient = other_grad.a[units:]
        total = attention_grad.a
        gain_parts = total[rows : rows + 2]
        triple_gradient = total[:rows].reshape(3, heads_width, -1).transpose(0, 2, 1)
        mixing_gradient = total[rows + 16 :]
    gain_parts = jnp.sum(lax.all_gather(gain_parts, "tp"), axis=0)
    lifting_gradient = lifting_gradient.transpose(2, 0, 1)
    triple_gradient = triple_gradient.transpose(1, 0, 2)

    return (
        output,
        input_gradient,
        gain_parts[0],
        triple_gradient,
        mixing_gradient,
        gain_parts[1],
        lifting_gradient,
        down_gradient,
    )


def solution(mesh):
    in_specs = (
        P("fsdp", "ctx", None),
        P("fsdp", "ctx", None),
        P("fsdp"),
        P("fsdp"),
        P("fsdp", None, "tp"),
        P("tp", "fsdp"),
        P("fsdp"),
        P("fsdp", None, "tp"),
        P("tp", "fsdp"),
    )
    out_specs = (
        P("fsdp", "ctx", None),
        P("fsdp", "ctx", None),
        P("fsdp"),
        P("fsdp", None, "tp"),
        P("tp", "fsdp"),
        P("fsdp"),
        P("fsdp", None, "tp"),
        P("tp", "fsdp"),
    )
    return jax.shard_map(
        functools.partial(on_device, sizes=dict(mesh.shape)),
        mesh=mesh,
        in_specs=in_specs,
        out_specs=out_specs,
        check_vma=False,
    )
```

profile of v0, /device:TPU:0, one launch (start us, length us, event | category | flops | bytes accessed | tf_op | source)
XLA Modules:
  0.0 330.0 jit_solution(7117243504523431180)
XLA Ops:
  2.7 2.9 collective-permute-start
  12.9 3.9 %collective-permute-done.1.refs_5_.refs_9_ = bf16[512,256]{1,0:T(8,128)(2,1)S(1)} collective-permute-done((bf16[512,256]{1,0:T(8,128)(2,1)S(1)}, bf16[512,256]{1,0:T(8,128)(2,1)S(1)}, u32[]{:S(2)}, u32[]{:S(2)}) %collective-permute-start.1) | collective-permute-done | bytes 262176 | tf_op jit(solution)/shard_map/ppermute | solution.py:49
  19.8 2.6 collective-permute-start.3
  22.8 5.2 %collective-permute-done.6.refs_7_.refs_11_ = bf16[512,256]{1,0:T(8,128)(2,1)S(1)} collective-permute-done((bf16[512,256]{1,0:T(8,128)(2,1)S(1)}, bf16[512,256]{1,0:T(8,128)(2,1)S(1)}, u32[]{:S(2)}, u32[]{:S(2)}) %collective-permute-start.6) | collective-permute-done | bytes 262176 | tf_op jit(solution)/shard_map/ppermute | solution.py:49
  31.0 2.6 collective-permute-start.8
  36.3 2.6 collective-permute-start.14
  38.8 4.0 %collective-permute-start.15 = (bf16[128,512]{1,0:T(8,128)(2,1)S(1)}, bf16[128,512]{1,0:T(8,128)(2,1)S(1)}, u32[]{:S(2)}, u32[]{:S(2)}) collective-permute-start(bf16[128,512]{1,0:T(8,128)(2,1)S(1)} %get-tuple-element.127), channel_id=1, source_target_pairs={{0,8},{4,12},{8,0},{12,4},{1,9},{5,13},{9,1},{13,5},{2,10},{6,14},... | collective-permute-start | bytes 393224 | tf_op jit(solution)/shard_map/ppermute | solution.py:49
  46.5 8.8 %attend.2 = (bf16[64,512]{1,0:T(8,128)(2,1)S(1)}, bf16[64,512]{1,0:T(8,128)(2,1)S(1)}, bf16[64,512]{1,0:T(8,128)(2,1)S(1)}, bf16[64,512]{1,0:T(8,128)(2,1)S(1)},...) custom-call(s32[5]{0:T(128)S(1)} %stack.47.refs_0_, s32[2]{0:T(128)S(1)} %copy-done.5, ...), custom_call_target="tpu_custom_call" | custom-call | flops 8808920064 | tf_op jit(solution)/shard_map/attend/pallas_call | solution.py:83
  55.4 3.1 collective-permute-start.11
  60.9 18.2 %attend.3 = (bf16[64,512]{1,0:T(8,128)(2,1)S(1)}, bf16[64,512]{1,0:T(8,128)(2,1)S(1)}, bf16[64,512]{1,0:T(8,128)(2,1)S(1)}, bf16[64,512]{1,0:T(8,128)(2,1)S(1)},...) custom-call(s32[5]{0:T(128)S(1)} %stack.47.refs_0_, s32[2]{0:T(128)S(1)} %copy-done.5, ...), custom_call_target="tpu_custom_call" | custom-call | flops 8808920064 | tf_op jit(solution)/shard_map/attend/pallas_call | solution.py:83
  80.2 2.2 all_gather.18.refs_1_.refs_8_
  89.9 3.4 %collective-permute-done.24.refs_3_ = bf16[64,512]{1,0:T(8,128)(2,1)S(1)} collective-permute-done((bf16[64,512]{1,0:T(8,128)(2,1)S(1)}, bf16[64,512]{1,0:T(8,128)(2,1)S(1)}, u32[]{:S(2)}, u32[]{:S(2)}) %collective-permute-start.24) | collective-permute-done | bytes 65568 | tf_op jit(solution)/shard_map/ppermute | solution.py:49
  93.9 2.2 all_gather.19.refs_1_.refs_9_
  98.7 4.4 %collective-permute-done.19.refs_2_ = bf16[256,1024]{1,0:T(8,128)(2,1)S(1)} collective-permute-done((bf16[256,1024]{1,0:T(8,128)(2,1)S(1)}, bf16[256,1024]{1,0:T(8,128)(2,1)S(1)}, u32[]{:S(2)}, u32[]{:S(2)}) %collective-permute-start.19) | collective-permute-done | bytes 524320 | tf_op jit(solution)/shard_map/ppermute | solution.py:49
  103.1 6.6 %feed.2 = (f32[256,1024]{1,0:T(8,128)S(1)}, bf16[256,1024]{1,0:T(8,128)(2,1)S(1)}, bf16[256,1024]{1,0:T(8,128)(2,1)S(1)}, bf16[256,3328]{1,0:T(8,128)(2,1)S(1)}, bf16[256,3328]{1,0:T(8,128)(2,1)S(1)}) custom-call(s32[5]{0:T(128)S(1)} %stack.47.refs_0_, bf16[256,1024]{1,0:T(8,128)(2,1)S(1)} %mix.2.refs_5_.refs_1_, ...), custom_call_target="tpu_custom_call" | custom-call | flops 3501545728 | tf_op jit(solution)/shard_map/feed/pallas_call | solution.py:83
  111.3 3.1 collective-permute-done.26.refs_2_
  114.3 6.6 %feed.3 = (f32[256,1024]{1,0:T(8,128)S(1)}, bf16[256,1024]{1,0:T(8,128)(2,1)S(1)}, bf16[256,1024]{1,0:T(8,128)(2,1)S(1)}, bf16[256,3328]{1,0:T(8,128)(2,1)S(1)}, bf16[256,3328]{1,0:T(8,128)(2,1)S(1)}) custom-call(s32[5]{0:T(128)S(1)} %stack.47.refs_0_, bf16[256,1024]{1,0:T(8,128)(2,1)S(1)} %mix.3.refs_10_.refs_1_, ...), custom_call_target="tpu_custom_call" | custom-call | flops 3501545728 | tf_op jit(solution)/shard_map/feed/pallas_call | solution.py:83
  122.5 3.1 collective-permute-done.28.refs_2_
  127.5 2.4 all_gather.20.refs_1_
  130.6 2.9 collective-permute-start.32
  139.7 12.9 %attend_back.2 = (bf16[192,512]{1,0:T(8,128)(2,1)S(1)}, bf16[192,512]{1,0:T(8,128)(2,1)S(1)}, bf16[192,512]{1,0:T(8,128)(2,1)S(1)}, bf16[192,512]{1,0:T(8,128)(2,1)S(1)}) custom-call(s32[5]{0:T(128)S(1)} %stack.47.refs_0_, s32[2]{0:T(128)S(1)} %copy-done.5, bf16[64,1024]{1,0:T(8,128)(2,1)S(1)} %get-tuple-element.110.refs_9_.refs_2_, ...), custom_call_target="tpu_custom_call" | custom-call | flops 22850338816 | tf_op jit(solution)/shard_map/attend_back/pallas_call | solution.py:83
  152.6 2.1 feed_grad1.1
  154.8 2.6 all_gather.21.refs_1_
  163.0 3.5 %feed_grad2.1 = (f32[1312,512]{1,0:T(8,128)S(1)}, bf16[1312,512]{1,0:T(8,128)(2,1)S(1)}) custom-call(s32[5]{0:T(128)S(1)} %stack.47.refs_0_, bf16[256,3328]{1,0:T(8,128)(2,1)S(1)} %get-tuple-element.150.refs_1_, bf16[256,3328]{1,0:T(8,128)(2,1)S(1)} %collective-permute-done.29.refs_2_, bf16[256,3328]{1,0:T(8,128)(2,1)S(1)} %get-tuple-element.154.refs_3_, ...), custom_call_target="tpu_custom_call" | custom-call | flops 2995032832 | tf_op jit(solution)/shard_map/feed_grad2/pallas_call | solution.py:83
  166.5 3.6 %collective-permute-done.37.refs_2_ = bf16[656,512]{1,0:T(8,128)(2,1)S(1)} collective-permute-done((bf16[656,512]{1,0:T(8,128)(2,1)S(1)}, bf16[656,512]{1,0:T(8,128)(2,1)S(1)}, u32[]{:S(2)}, u32[]{:S(2)}) %collective-permute-start.37) | collective-permute-done | bytes 671776 | tf_op jit(solution)/shard_map/ppermute | solution.py:49
  170.1 2.1 collective-permute-start.36
  174.7 6.9 %collective-permute-start.46 = (bf16[1312,512]{1,0:T(8,128)(2,1)S(1)}, bf16[1312,512]{1,0:T(8,128)(2,1)S(1)}, u32[]{:S(2)}, u32[]{:S(2)}) collective-permute-start(bf16[1312,512]{1,0:T(8,128)(2,1)S(1)} %get-tuple-element.182), channel_id=1, source_target_pairs={{0,16},{16,0},{1,17},{17,1},{2,18},{18,2},{3,19},{19,3},{4,20},{20... | collective-permute-start | bytes 4030472 | tf_op jit(solution)/shard_map/ppermute | solution.py:49
  181.6 12.8 %attend_back.3 = (bf16[192,512]{1,0:T(8,128)(2,1)S(1)}, bf16[192,512]{1,0:T(8,128)(2,1)S(1)}, bf16[192,512]{1,0:T(8,128)(2,1)S(1)}, bf16[192,512]{1,0:T(8,128)(2,1)S(1)}) custom-call(s32[5]{0:T(128)S(1)} %stack.47.refs_0_, s32[2]{0:T(128)S(1)} %copy-done.5, bf16[64,1024]{1,0:T(8,128)(2,1)S(1)} %get-tuple-element.110.refs_9_.refs_2_, ...), custom_call_target="tpu_custom_call" | custom-call | flops 22850338816 | tf_op jit(solution)/shard_map/attend_back/pallas_call | solution.py:83
  206.0 3.5 %collective-permute-done.39.refs_3_ = bf16[192,512]{1,0:T(8,128)(2,1)S(1)} collective-permute-done((bf16[192,512]{1,0:T(8,128)(2,1)S(1)}, bf16[192,512]{1,0:T(8,128)(2,1)S(1)}, u32[]{:S(2)}, u32[]{:S(2)}) %collective-permute-start.39) | collective-permute-done | bytes 196640 | tf_op jit(solution)/shard_map/ppermute | solution.py:49
  209.4 7.5 %collective-permute-start.52 = (bf16[1312,256]{1,0:T(8,128)(2,1)S(1)}, bf16[1312,256]{1,0:T(8,128)(2,1)S(1)}, u32[]{:S(2)}, u32[]{:S(2)}) collective-permute-start(bf16[1312,256]{1,0:T(8,128)(2,1)S(1)} %get-tuple-element.197), channel_id=1, source_target_pairs={{0,4},{4,0},{8,12},{12,8},{1,5},{5,1},{9,13},{13,9},{2,6},{6,2},{1... | collective-permute-start | bytes 2015240 | tf_op jit(solution)/shard_map/ppermute | solution.py:49
  220.4 2.9 attention_grad.1
  223.3 2.4 collective-permute-start.55
  225.9 2.1 collective-permute-start.57
  230.8 2.4 collective-permute-start.54
  233.2 7.5 %collective-permute-done.57.refs_2_ = bf16[256,1024]{1,0:T(8,128)(2,1)S(1)} collective-permute-done((bf16[256,1024]{1,0:T(8,128)(2,1)S(1)}, bf16[256,1024]{1,0:T(8,128)(2,1)S(1)}, u32[]{:S(2)}, u32[]{:S(2)}) %collective-permute-start.57) | collective-permute-done | bytes 524320 | tf_op jit(solution)/shard_map/ppermute | solution.py:49
  242.1 4.7 %collective-permute-done.56.refs_2_ = bf16[656,128]{1,0:T(8,128)(2,1)S(1)} collective-permute-done((bf16[656,128]{1,0:T(8,128)(2,1)S(1)}, bf16[656,128]{1,0:T(8,128)(2,1)S(1)}, u32[]{:S(2)}, u32[]{:S(2)}) %collective-permute-start.56) | collective-permute-done | bytes 167968 | tf_op jit(solution)/shard_map/ppermute | solution.py:49
  247.5 2.4 collective-permute-done.55.refs_2_
  255.3 7.5 %collective-permute-done.51.refs_5_ = bf16[2,256,1024]{2,1,0:T(8,128)(2,1)S(1)} collective-permute-done((bf16[2,256,1024]{2,1,0:T(8,128)(2,1)S(1)}, bf16[2,256,1024]{2,1,0:T(8,128)(2,1)S(1)}, u32[]{:S(2)}, u32[]{:S(2)}) %collective-permute-start.51) | collective-permute-done | bytes 1048608 | tf_op jit(solution)/shard_map/ppermute | solution.py:49
  263.8 8.1 %collective-permute-done.59.refs_2_ = bf16[1040,256]{1,0:T(8,128)(2,1)S(1)} collective-permute-done((bf16[1040,256]{1,0:T(8,128)(2,1)S(1)}, bf16[1040,256]{1,0:T(8,128)(2,1)S(1)}, u32[]{:S(2)}, u32[]{:S(2)}) %collective-permute-start.59) | collective-permute-done | bytes 532512 | tf_op jit(solution)/shard_map/ppermute | solution.py:49
  274.7 2.5 collective-permute-start.67
  279.3 7.4 %collective-permute-done.60.refs_1_ = bf16[1040,128]{1,0:T(8,128)(2,1)S(1)} collective-permute-done((bf16[1040,128]{1,0:T(8,128)(2,1)S(1)}, bf16[1040,128]{1,0:T(8,128)(2,1)S(1)}, u32[]{:S(2)}, u32[]{:S(2)}) %collective-permute-start.60) | collective-permute-done | bytes 266272 | tf_op jit(solution)/shard_map/ppermute | solution.py:49
  288.5 2.8 collective-permute-start.66
  291.3 10.5 %collective-permute-done.64.refs_2_ = bf16[1040,128]{1,0:T(8,128)(2,1)S(1)} collective-permute-done((bf16[1040,128]{1,0:T(8,128)(2,1)S(1)}, bf16[1040,128]{1,0:T(8,128)(2,1)S(1)}, u32[]{:S(2)}, u32[]{:S(2)}) %collective-permute-start.64) | collective-permute-done | bytes 266272 | tf_op jit(solution)/shard_map/ppermute | solution.py:49
  302.4 2.3 collective-permute-start.65
  306.7 4.4 %collective-permute-done.66.refs_2_ = bf16[656,256]{1,0:T(8,128)(2,1)S(1)} collective-permute-done((bf16[656,256]{1,0:T(8,128)(2,1)S(1)}, bf16[656,256]{1,0:T(8,128)(2,1)S(1)}, u32[]{:S(2)}, u32[]{:S(2)}) %collective-permute-start.66) | collective-permute-done | bytes 335904 | tf_op jit(solution)/shard_map/ppermute | solution.py:49
  312.7 2.7 feed_end.1
  315.5 5.1 %collective-permute-done.65.refs_2_ = bf16[1040,256]{1,0:T(8,128)(2,1)S(1)} collective-permute-done((bf16[1040,256]{1,0:T(8,128)(2,1)S(1)}, bf16[1040,256]{1,0:T(8,128)(2,1)S(1)}, u32[]{:S(2)}, u32[]{:S(2)}) %collective-permute-start.65) | collective-permute-done | bytes 532512 | tf_op jit(solution)/shard_map/ppermute | solution.py:49
  324.0 5.3 %all-gather.1 = f32[4,2,512]{2,1,0:T(2,128)S(1)} all-gather(f32[1,2,512]{2,1,0:T(2,128)S(1)} %bitcast.28), channel_id=2, replica_groups=mesh['fsdp'=2,'ctx'=4,'tp'=4] {'tp'}, dimensions={0}, use_global_device_ids=true | all-gather | bytes 20480 | tf_op jit(solution)/shard_map/all_gather | solution.py:950
  (174 shorter events, 97.3 us)
Async XLA Ops:
  12.8 15.2 %collective-permute-start.6 = (bf16[512,256]{1,0:T(8,128)(2,1)S(1)}, bf16[512,256]{1,0:T(8,128)(2,1)S(1)}, u32[]{:S(2)}, u32[]{:S(2)}) collective-permute-start(bf16[512,256]{1,0:T(8,128)(2,1)S(1)} %get-tuple-element.115.refs_6_.refs_10_), channel_id=1, source_target_pairs={{0,16},{16,0},{1,17},{17,1},{2,18},{18,2},{3,19},{19,3},{4,20},{20... | collective-permute-start | bytes 786440 | tf_op jit(solution)/shard_map/ppermute | solution.py:49
  19.8 13.8 %collective-permute-start.3 = (bf16[64,1024]{1,0:T(8,128)(2,1)S(1)}, bf16[64,1024]{1,0:T(8,128)(2,1)S(1)}, u32[]{:S(2)}, u32[]{:S(2)}) collective-permute-start(bf16[64,1024]{1,0:T(8,128)(2,1)S(1)} %get-tuple-element.112), channel_id=1, source_target_pairs={{0,8},{4,12},{8,0},{12,4},{1,9},{5,13},{9,1},{13,5},{2,10},{6,14},... | collective-permute-start | bytes 393224 | tf_op jit(solution)/shard_map/ppermute | solution.py:49
  31.0 13.5 %collective-permute-start.8 = (bf16[128,512]{1,0:T(8,128)(2,1)S(1)}, bf16[128,512]{1,0:T(8,128)(2,1)S(1)}, u32[]{:S(2)}, u32[]{:S(2)}) collective-permute-start(bf16[128,512]{1,0:T(8,128)(2,1)S(1)} %get-tuple-element.118), channel_id=1, source_target_pairs={{0,8},{4,12},{8,0},{12,4},{1,9},{5,13},{9,1},{13,5},{2,10},{6,14},... | collective-permute-start | bytes 393224 | tf_op jit(solution)/shard_map/ppermute | solution.py:49
  33.6 12.9 %collective-permute-start.9 = (bf16[128,512]{1,0:T(8,128)(2,1)S(1)}, bf16[128,512]{1,0:T(8,128)(2,1)S(1)}, u32[]{:S(2)}, u32[]{:S(2)}) collective-permute-start(bf16[128,512]{1,0:T(8,128)(2,1)S(1)} %get-tuple-element.119), channel_id=1, source_target_pairs={{0,12},{4,8},{8,4},{12,0},{1,13},{5,9},{9,5},{13,1},{2,14},{6,10},... | collective-permute-start | bytes 393224 | tf_op jit(solution)/shard_map/ppermute | solution.py:49
  34.0 49.6 %collective-permute-start.20 = (bf16[1968,512]{1,0:T(8,128)(2,1)S(1)}, bf16[1968,512]{1,0:T(8,128)(2,1)S(1)}, u32[]{:S(2)}, u32[]{:S(2)}) collective-permute-start(bf16[1968,512]{1,0:T(8,128)(2,1)S(1)} %pad_maximum_fusion.refs_6_), channel_id=1, source_target_pairs={{0,16},{16,0},{1,17},{17,1},{2,18},{18,2},{3,19},{19,3},{4,20},{20... | collective-permute-start | bytes 6045704 | tf_op jit(solution)/shard_map/ppermute | solution.py:49
  36.3 22.1 %collective-permute-start.14 = (bf16[128,512]{1,0:T(8,128)(2,1)S(1)}, bf16[128,512]{1,0:T(8,128)(2,1)S(1)}, u32[]{:S(2)}, u32[]{:S(2)}) collective-permute-start(bf16[128,512]{1,0:T(8,128)(2,1)S(1)} %get-tuple-element.126), channel_id=1, source_target_pairs={{0,4},{4,0},{8,12},{12,8},{1,5},{5,1},{9,13},{13,9},{2,6},{6,2},{1... | collective-permute-start | bytes 393224 | tf_op jit(solution)/shard_map/ppermute | solution.py:49
  38.8 20.4 %collective-permute-start.15 = (bf16[128,512]{1,0:T(8,128)(2,1)S(1)}, bf16[128,512]{1,0:T(8,128)(2,1)S(1)}, u32[]{:S(2)}, u32[]{:S(2)}) collective-permute-start(bf16[128,512]{1,0:T(8,128)(2,1)S(1)} %get-tuple-element.127), channel_id=1, source_target_pairs={{0,8},{4,12},{8,0},{12,4},{1,9},{5,13},{9,1},{13,5},{2,10},{6,14},... | collective-permute-start | bytes 393224 | tf_op jit(solution)/shard_map/ppermute | solution.py:49
  44.5 16.4 %collective-permute-start.16 = (bf16[128,512]{1,0:T(8,128)(2,1)S(1)}, bf16[128,512]{1,0:T(8,128)(2,1)S(1)}, u32[]{:S(2)}, u32[]{:S(2)}) collective-permute-start(bf16[128,512]{1,0:T(8,128)(2,1)S(1)} %get-tuple-element.128), channel_id=1, source_target_pairs={{0,12},{4,8},{8,4},{12,0},{1,13},{5,9},{9,5},{13,1},{2,14},{6,10},... | collective-permute-start | bytes 393224 | tf_op jit(solution)/shard_map/ppermute | solution.py:49
  55.4 23.7 %collective-permute-start.11 = (bf16[64,512]{1,0:T(8,128)(2,1)S(1)}, bf16[64,512]{1,0:T(8,128)(2,1)S(1)}, u32[]{:S(2)}, u32[]{:S(2)}) collective-permute-start(bf16[64,512]{1,0:T(8,128)(2,1)S(1)} %get-tuple-element.123), channel_id=1, source_target_pairs={{0,4},{4,0},{8,12},{12,8},{1,5},{5,1},{9,13},{13,9},{2,6},{6,2},{1... | collective-permute-start | bytes 196616 | tf_op jit(solution)/shard_map/ppermute | solution.py:49
  58.4 20.6 %collective-permute-start.12 = (bf16[64,512]{1,0:T(8,128)(2,1)S(1)}, bf16[64,512]{1,0:T(8,128)(2,1)S(1)}, u32[]{:S(2)}, u32[]{:S(2)}) collective-permute-start(bf16[64,512]{1,0:T(8,128)(2,1)S(1)} %get-tuple-element.124), channel_id=1, source_target_pairs={{0,8},{4,12},{8,0},{12,4},{1,9},{5,13},{9,1},{13,5},{2,10},{6,14},... | collective-permute-start | bytes 196616 | tf_op jit(solution)/shard_map/ppermute | solution.py:49
  59.3 19.8 %collective-permute-start.13 = (bf16[64,512]{1,0:T(8,128)(2,1)S(1)}, bf16[64,512]{1,0:T(8,128)(2,1)S(1)}, u32[]{:S(2)}, u32[]{:S(2)}) collective-permute-start(bf16[64,512]{1,0:T(8,128)(2,1)S(1)} %get-tuple-element.125), channel_id=1, source_target_pairs={{0,12},{4,8},{8,4},{12,0},{1,13},{5,9},{9,5},{13,1},{2,14},{6,10},... | collective-permute-start | bytes 196616 | tf_op jit(solution)/shard_map/ppermute | solution.py:49
  83.4 19.7 %collective-permute-start.21 = (bf16[1968,512]{1,0:T(8,128)(2,1)S(1)}, bf16[1968,512]{1,0:T(8,128)(2,1)S(1)}, u32[]{:S(2)}, u32[]{:S(2)}) collective-permute-start(bf16[1968,512]{1,0:T(8,128)(2,1)S(1)} %pad_maximum_fusion.refs_6_), channel_id=1, source_target_pairs={{0,1},{1,0},{2,3},{3,2},{4,5},{5,4},{6,7},{7,6},{8,9},{9,8},{10,11... | collective-permute-start | bytes 6045704 | tf_op jit(solution)/shard_map/ppermute | solution.py:49
  83.6 19.5 %collective-permute-start.22 = (bf16[1968,512]{1,0:T(8,128)(2,1)S(1)}, bf16[1968,512]{1,0:T(8,128)(2,1)S(1)}, u32[]{:S(2)}, u32[]{:S(2)}) collective-permute-start(bf16[1968,512]{1,0:T(8,128)(2,1)S(1)} %collective-permute-done.20.refs_7_), channel_id=1, source_target_pairs={{0,1},{1,0},{2,3},{3,2},{4,5},{5,4},{6,7},{7,6},{8,9},{9,8},{10,11... | collective-permute-start | bytes 6045704 | tf_op jit(solution)/shard_map/ppermute | solution.py:49
  88.4 14.7 %collective-permute-start.19 = (bf16[256,1024]{1,0:T(8,128)(2,1)S(1)}, bf16[256,1024]{1,0:T(8,128)(2,1)S(1)}, u32[]{:S(2)}, u32[]{:S(2)}) collective-permute-start(bf16[256,1024]{1,0:T(8,128)(2,1)S(1)} %mix.2.refs_5_.refs_1_), channel_id=1, source_target_pairs={{0,2},{1,3},{2,0},{3,1},{4,6},{5,7},{6,4},{7,5},{8,10},{9,11},{10,... | collective-permute-start | bytes 1572872 | tf_op jit(solution)/shard_map/ppermute | solution.py:49
  97.1 17.2 %collective-permute-start.26 = (bf16[256,1024]{1,0:T(8,128)(2,1)S(1)}, bf16[256,1024]{1,0:T(8,128)(2,1)S(1)}, u32[]{:S(2)}, u32[]{:S(2)}) collective-permute-start(bf16[256,1024]{1,0:T(8,128)(2,1)S(1)} %mix.3.refs_10_.refs_1_), channel_id=1, source_target_pairs={{0,2},{1,3},{2,0},{3,1},{4,6},{5,7},{6,4},{7,5},{8,10},{9,11},{10,... | collective-permute-start | bytes 1572872 | tf_op jit(solution)/shard_map/ppermute | solution.py:49
  109.7 15.9 %collective-permute-start.28 = (bf16[256,1024]{1,0:T(8,128)(2,1)S(1)}, bf16[256,1024]{1,0:T(8,128)(2,1)S(1)}, u32[]{:S(2)}, u32[]{:S(2)}) collective-permute-start(bf16[256,1024]{1,0:T(8,128)(2,1)S(1)} %get-tuple-element.145.refs_1_), channel_id=1, source_target_pairs={{0,2},{1,3},{2,0},{3,1},{4,6},{5,7},{6,4},{7,5},{8,10},{9,11},{10,... | collective-permute-start | bytes 1572872 | tf_op jit(solution)/shard_map/ppermute | solution.py:49
  120.9 14.3 %collective-permute-start.27 = (bf16[256,1024]{1,0:T(8,128)(2,1)S(1)}, bf16[256,1024]{1,0:T(8,128)(2,1)S(1)}, u32[]{:S(2)}, u32[]{:S(2)}) collective-permute-start(bf16[256,1024]{1,0:T(8,128)(2,1)S(1)} %get-tuple-element.144.refs_1_), channel_id=1, source_target_pairs={{0,2},{1,3},{2,0},{3,1},{4,6},{5,7},{6,4},{7,5},{8,10},{9,11},{10,... | collective-permute-start | bytes 1572872 | tf_op jit(solution)/shard_map/ppermute | solution.py:49
  137.2 15.3 %collective-permute-start.29 = (bf16[256,3328]{1,0:T(8,128)(2,1)S(1)}, bf16[256,3328]{1,0:T(8,128)(2,1)S(1)}, u32[]{:S(2)}, u32[]{:S(2)}) collective-permute-start(bf16[256,3328]{1,0:T(8,128)(2,1)S(1)} %get-tuple-element.153), channel_id=1, source_target_pairs={{0,1},{1,0},{2,3},{3,2},{4,5},{5,4},{6,7},{7,6},{8,9},{9,8},{10,11... | collective-permute-start | bytes 5111816 | tf_op jit(solution)/shard_map/ppermute | solution.py:49
  137.3 15.3 %collective-permute-start.30 = (bf16[256,3328]{1,0:T(8,128)(2,1)S(1)}, bf16[256,3328]{1,0:T(8,128)(2,1)S(1)}, u32[]{:S(2)}, u32[]{:S(2)}) collective-permute-start(bf16[256,3328]{1,0:T(8,128)(2,1)S(1)} %get-tuple-element.156), channel_id=1, source_target_pairs={{0,1},{1,0},{2,3},{3,2},{4,5},{5,4},{6,7},{7,6},{8,9},{9,8},{10,11... | collective-permute-start | bytes 5111816 | tf_op jit(solution)/shard_map/ppermute | solution.py:49
  154.7 15.4 %collective-permute-start.37 = (bf16[656,512]{1,0:T(8,128)(2,1)S(1)}, bf16[656,512]{1,0:T(8,128)(2,1)S(1)}, u32[]{:S(2)}, u32[]{:S(2)}) collective-permute-start(bf16[656,512]{1,0:T(8,128)(2,1)S(1)} %get-tuple-element.168), channel_id=1, source_target_pairs={{0,16},{16,0},{1,17},{17,1},{2,18},{18,2},{3,19},{19,3},{4,20},{20... | collective-permute-start | bytes 2015240 | tf_op jit(solution)/shard_map/ppermute | solution.py:49
  157.4 39.8 %collective-permute-start.41 = (bf16[192,512]{1,0:T(8,128)(2,1)S(1)}, bf16[192,512]{1,0:T(8,128)(2,1)S(1)}, u32[]{:S(2)}, u32[]{:S(2)}) collective-permute-start(bf16[192,512]{1,0:T(8,128)(2,1)S(1)} %get-tuple-element.175), channel_id=1, source_target_pairs={{0,4},{4,0},{8,12},{12,8},{1,5},{5,1},{9,13},{13,9},{2,6},{6,2},{1... | collective-permute-start | bytes 589832 | tf_op jit(solution)/shard_map/ppermute | solution.py:49
  158.3 39.8 %collective-permute-start.42 = (bf16[192,512]{1,0:T(8,128)(2,1)S(1)}, bf16[192,512]{1,0:T(8,128)(2,1)S(1)}, u32[]{:S(2)}, u32[]{:S(2)}) collective-permute-start(bf16[192,512]{1,0:T(8,128)(2,1)S(1)} %get-tuple-element.176), channel_id=1, source_target_pairs={{0,8},{4,12},{8,0},{12,4},{1,9},{5,13},{9,1},{13,5},{2,10},{6,14},... | collective-permute-start | bytes 589832 | tf_op jit(solution)/shard_map/ppermute | solution.py:49
  160.4 12.5 %collective-permute-start.34 = (bf16[64,512]{1,0:T(8,128)(2,1)S(1)}, bf16[64,512]{1,0:T(8,128)(2,1)S(1)}, u32[]{:S(2)}, u32[]{:S(2)}) collective-permute-start(bf16[64,512]{1,0:T(8,128)(2,1)S(1)} %get-tuple-element.164), channel_id=1, source_target_pairs={{0,4},{4,0},{8,12},{12,8},{1,5},{5,1},{9,13},{13,9},{2,6},{6,2},{1... | collective-permute-start | bytes 196616 | tf_op jit(solution)/shard_map/ppermute | solution.py:49
  161.7 13.0 %collective-permute-start.35 = (bf16[64,512]{1,0:T(8,128)(2,1)S(1)}, bf16[64,512]{1,0:T(8,128)(2,1)S(1)}, u32[]{:S(2)}, u32[]{:S(2)}) collective-permute-start(bf16[64,512]{1,0:T(8,128)(2,1)S(1)} %get-tuple-element.165), channel_id=1, source_target_pairs={{0,8},{4,12},{8,0},{12,4},{1,9},{5,13},{9,1},{13,5},{2,10},{6,14},... | collective-permute-start | bytes 196616 | tf_op jit(solution)/shard_map/ppermute | solution.py:49
  172.9 26.8 %collective-permute-start.43 = (bf16[192,512]{1,0:T(8,128)(2,1)S(1)}, bf16[192,512]{1,0:T(8,128)(2,1)S(1)}, u32[]{:S(2)}, u32[]{:S(2)}) collective-permute-start(bf16[192,512]{1,0:T(8,128)(2,1)S(1)} %get-tuple-element.177), channel_id=1, source_target_pairs={{0,12},{4,8},{8,4},{12,0},{1,13},{5,9},{9,5},{13,1},{2,14},{6,10},... | collective-permute-start | bytes 589832 | tf_op jit(solution)/shard_map/ppermute | solution.py:49
  174.7 28.2 %collective-permute-start.46 = (bf16[1312,512]{1,0:T(8,128)(2,1)S(1)}, bf16[1312,512]{1,0:T(8,128)(2,1)S(1)}, u32[]{:S(2)}, u32[]{:S(2)}) collective-permute-start(bf16[1312,512]{1,0:T(8,128)(2,1)S(1)} %get-tuple-element.182), channel_id=1, source_target_pairs={{0,16},{16,0},{1,17},{17,1},{2,18},{18,2},{3,19},{19,3},{4,20},{20... | collective-permute-start | bytes 4030472 | tf_op jit(solution)/shard_map/ppermute | solution.py:49
  181.6 12.9 %collective-permute-start.44 = (bf16[656,256]{1,0:T(8,128)(2,1)S(1)}, bf16[656,256]{1,0:T(8,128)(2,1)S(1)}, u32[]{:S(2)}, u32[]{:S(2)}) collective-permute-start(bf16[656,256]{1,0:T(8,128)(2,1)S(1)} %get-tuple-element.178), channel_id=1, source_target_pairs={{0,4},{4,0},{8,12},{12,8},{1,5},{5,1},{9,13},{13,9},{2,6},{6,2},{1... | collective-permute-start | bytes 1007624 | tf_op jit(solution)/shard_map/ppermute | solution.py:49
  197.2 12.2 %collective-permute-start.39 = (bf16[192,512]{1,0:T(8,128)(2,1)S(1)}, bf16[192,512]{1,0:T(8,128)(2,1)S(1)}, u32[]{:S(2)}, u32[]{:S(2)}) collective-permute-start(bf16[192,512]{1,0:T(8,128)(2,1)S(1)} %get-tuple-element.173), channel_id=1, source_target_pairs={{0,8},{4,12},{8,0},{12,4},{1,9},{5,13},{9,1},{13,5},{2,10},{6,14},... | collective-permute-start | bytes 589832 | tf_op jit(solution)/shard_map/ppermute | solution.py:49
  203.9 15.1 %collective-permute-start.50 = (bf16[256,1024]{1,0:T(8,128)(2,1)S(1)}, bf16[256,1024]{1,0:T(8,128)(2,1)S(1)}, u32[]{:S(2)}, u32[]{:S(2)}) collective-permute-start(bf16[256,1024]{1,0:T(8,128)(2,1)S(1)} %project_sum.2.refs_12_.refs_1_), channel_id=1, source_target_pairs={{0,2},{1,3},{2,0},{3,1},{4,6},{5,7},{6,4},{7,5},{8,10},{9,11},{10,... | collective-permute-start | bytes 1572872 | tf_op jit(solution)/shard_map/ppermute | solution.py:49
  205.4 14.9 %collective-permute-start.48 = (bf16[256,1024]{1,0:T(8,128)(2,1)S(1)}, bf16[256,1024]{1,0:T(8,128)(2,1)S(1)}, u32[]{:S(2)}, u32[]{:S(2)}) collective-permute-start(bf16[256,1024]{1,0:T(8,128)(2,1)S(1)} %get-tuple-element.191.refs_10_), channel_id=1, source_target_pairs={{0,1},{1,0},{2,3},{3,2},{4,5},{5,4},{6,7},{7,6},{8,9},{9,8},{10,11... | collective-permute-start | bytes 1572872 | tf_op jit(solution)/shard_map/ppermute | solution.py:49
  205.5 14.9 %collective-permute-start.49 = (bf16[256,1024]{1,0:T(8,128)(2,1)S(1)}, bf16[256,1024]{1,0:T(8,128)(2,1)S(1)}, u32[]{:S(2)}, u32[]{:S(2)}) collective-permute-start(bf16[256,1024]{1,0:T(8,128)(2,1)S(1)} %get-tuple-element.193.refs_12_), channel_id=1, source_target_pairs={{0,1},{1,0},{2,3},{3,2},{4,5},{5,4},{6,7},{7,6},{8,9},{9,8},{10,11... | collective-permute-start | bytes 1572872 | tf_op jit(solution)/shard_map/ppermute | solution.py:49
  209.4 18.6 %collective-permute-start.53 = (bf16[656,128]{1,0:T(8,128)(2,1)S(1)}, bf16[656,128]{1,0:T(8,128)(2,1)S(1)}, u32[]{:S(2)}, u32[]{:S(2)}) collective-permute-start(bf16[656,128]{1,0:T(8,128)(2,1)S(1)} %get-tuple-element.198), channel_id=1, source_target_pairs={{0,8},{4,12},{8,0},{12,4},{1,9},{5,13},{9,1},{13,5},{2,10},{6,14},... | collective-permute-start | bytes 503816 | tf_op jit(solution)/shard_map/ppermute | solution.py:49
  209.4 20.7 %collective-permute-start.52 = (bf16[1312,256]{1,0:T(8,128)(2,1)S(1)}, bf16[1312,256]{1,0:T(8,128)(2,1)S(1)}, u32[]{:S(2)}, u32[]{:S(2)}) collective-permute-start(bf16[1312,256]{1,0:T(8,128)(2,1)S(1)} %get-tuple-element.197), channel_id=1, source_target_pairs={{0,4},{4,0},{8,12},{12,8},{1,5},{5,1},{9,13},{13,9},{2,6},{6,2},{1... | collective-permute-start | bytes 2015240 | tf_op jit(solution)/shard_map/ppermute | solution.py:49
  223.3 26.6 %collective-permute-start.55 = (bf16[1040,512]{1,0:T(8,128)(2,1)S(1)}, bf16[1040,512]{1,0:T(8,128)(2,1)S(1)}, u32[]{:S(2)}, u32[]{:S(2)}) collective-permute-start(bf16[1040,512]{1,0:T(8,128)(2,1)S(1)} %get-tuple-element.201), channel_id=1, source_target_pairs={{0,16},{16,0},{1,17},{17,1},{2,18},{18,2},{3,19},{19,3},{4,20},{20... | collective-permute-start | bytes 3194888 | tf_op jit(solution)/shard_map/ppermute | solution.py:49
  225.9 14.8 %collective-permute-start.57 = (bf16[256,1024]{1,0:T(8,128)(2,1)S(1)}, bf16[256,1024]{1,0:T(8,128)(2,1)S(1)}, u32[]{:S(2)}, u32[]{:S(2)}) collective-permute-start(bf16[256,1024]{1,0:T(8,128)(2,1)S(1)} %project_sum.3.refs_2_.refs_1_), channel_id=1, source_target_pairs={{0,2},{1,3},{2,0},{3,1},{4,6},{5,7},{6,4},{7,5},{8,10},{9,11},{10,... | collective-permute-start | bytes 1572872 | tf_op jit(solution)/shard_map/ppermute | solution.py:49
  228.1 18.7 %collective-permute-start.56 = (bf16[656,128]{1,0:T(8,128)(2,1)S(1)}, bf16[656,128]{1,0:T(8,128)(2,1)S(1)}, u32[]{:S(2)}, u32[]{:S(2)}) collective-permute-start(bf16[656,128]{1,0:T(8,128)(2,1)S(1)} %sum_ctx.3.refs_3_.refs_1_), channel_id=1, source_target_pairs={{0,8},{4,12},{8,0},{12,4},{1,9},{5,13},{9,1},{13,5},{2,10},{6,14},... | collective-permute-start | bytes 503816 | tf_op jit(solution)/shard_map/ppermute | solution.py:49
  230.1 32.7 %collective-permute-start.51 = (bf16[2,256,1024]{2,1,0:T(8,128)(2,1)S(1)}, bf16[2,256,1024]{2,1,0:T(8,128)(2,1)S(1)}, u32[]{:S(2)}, u32[]{:S(2)}) collective-permute-start(bf16[2,256,1024]{2,1,0:T(8,128)(2,1)S(1)} %pad_maximum_fusion.1), channel_id=1, source_target_pairs={{0,2},{1,3},{2,0},{3,1},{4,6},{5,7},{6,4},{7,5},{8,10},{9,11},{10,... | collective-permute-start | bytes 3145736 | tf_op jit(solution)/shard_map/ppermute | solution.py:49
  230.8 22.4 %collective-permute-start.54 = (bf16[1312,128]{1,0:T(8,128)(2,1)S(1)}, bf16[1312,128]{1,0:T(8,128)(2,1)S(1)}, u32[]{:S(2)}, u32[]{:S(2)}) collective-permute-start(bf16[1312,128]{1,0:T(8,128)(2,1)S(1)} %get-tuple-element.200), channel_id=1, source_target_pairs={{0,8},{4,12},{8,0},{12,4},{1,9},{5,13},{9,1},{13,5},{2,10},{6,14},... | collective-permute-start | bytes 1007624 | tf_op jit(solution)/shard_map/ppermute | solution.py:49
  250.7 21.2 %collective-permute-start.59 = (bf16[1040,256]{1,0:T(8,128)(2,1)S(1)}, bf16[1040,256]{1,0:T(8,128)(2,1)S(1)}, u32[]{:S(2)}, u32[]{:S(2)}) collective-permute-start(bf16[1040,256]{1,0:T(8,128)(2,1)S(1)} %get-tuple-element.204), channel_id=1, source_target_pairs={{0,4},{4,0},{8,12},{12,8},{1,5},{5,1},{9,13},{13,9},{2,6},{6,2},{1... | collective-permute-start | bytes 1597448 | tf_op jit(solution)/shard_map/ppermute | solution.py:49
  250.8 26.5 %collective-permute-start.61 = (bf16[256,1024]{1,0:T(8,128)(2,1)S(1)}, bf16[256,1024]{1,0:T(8,128)(2,1)S(1)}, u32[]{:S(2)}, u32[]{:S(2)}) collective-permute-start(bf16[256,1024]{1,0:T(8,128)(2,1)S(1)} %norm_first_back.2.refs_14_.refs_1_), channel_id=1, source_target_pairs={{0,1},{1,0},{2,3},{3,2},{4,5},{5,4},{6,7},{7,6},{8,9},{9,8},{10,11... | collective-permute-start | bytes 1572872 | tf_op jit(solution)/shard_map/ppermute | solution.py:49
  250.9 26.4 %collective-permute-start.62 = (bf16[256,1024]{1,0:T(8,128)(2,1)S(1)}, bf16[256,1024]{1,0:T(8,128)(2,1)S(1)}, u32[]{:S(2)}, u32[]{:S(2)}) collective-permute-start(bf16[256,1024]{1,0:T(8,128)(2,1)S(1)} %norm_first_back.3.refs_3_), channel_id=1, source_target_pairs={{0,1},{1,0},{2,3},{3,2},{4,5},{5,4},{6,7},{7,6},{8,9},{9,8},{10,11... | collective-permute-start | bytes 1572872 | tf_op jit(solution)/shard_map/ppermute | solution.py:49
  253.3 20.8 %collective-permute-start.63 = (bf16[1312,128]{1,0:T(8,128)(2,1)S(1)}, bf16[1312,128]{1,0:T(8,128)(2,1)S(1)}, u32[]{:S(2)}, u32[]{:S(2)}) collective-permute-start(bf16[1312,128]{1,0:T(8,128)(2,1)S(1)} %sum_ctx.4.refs_6_.refs_1_), channel_id=1, source_target_pairs={{0,8},{4,12},{8,0},{12,4},{1,9},{5,13},{9,1},{13,5},{2,10},{6,14},... | collective-permute-start | bytes 1007624 | tf_op jit(solution)/shard_map/ppermute | solution.py:49
  263.7 41.0 %collective-permute-start.58 = (bf16[2,256,1024]{2,1,0:T(8,128)(2,1)S(1)}, bf16[2,256,1024]{2,1,0:T(8,128)(2,1)S(1)}, u32[]{:S(2)}, u32[]{:S(2)}) collective-permute-start(bf16[2,256,1024]{2,1,0:T(8,128)(2,1)S(1)} %output.1.refs_3_.refs_1_), channel_id=1, source_target_pairs={{0,1},{1,0},{2,3},{3,2},{4,5},{5,4},{6,7},{7,6},{8,9},{9,8},{10,11... | collective-permute-start | bytes 3145736 | tf_op jit(solution)/shard_map/ppermute | solution.py:49
  272.6 14.1 %collective-permute-start.60 = (bf16[1040,128]{1,0:T(8,128)(2,1)S(1)}, bf16[1040,128]{1,0:T(8,128)(2,1)S(1)}, u32[]{:S(2)}, u32[]{:S(2)}) collective-permute-start(bf16[1040,128]{1,0:T(8,128)(2,1)S(1)} %get-tuple-element.206), channel_id=1, source_target_pairs={{0,8},{4,12},{8,0},{12,4},{1,9},{5,13},{9,1},{13,5},{2,10},{6,14},... | collective-permute-start | bytes 798728 | tf_op jit(solution)/shard_map/ppermute | solution.py:49
  274.7 36.4 %collective-permute-start.67 = (bf16[1312,256]{1,0:T(8,128)(2,1)S(1)}, bf16[1312,256]{1,0:T(8,128)(2,1)S(1)}, u32[]{:S(2)}, u32[]{:S(2)}) collective-permute-start(bf16[1312,256]{1,0:T(8,128)(2,1)S(1)} %unite.4.refs_5_.refs_3_), channel_id=1, source_target_pairs={{0,4},{4,0},{8,12},{12,8},{1,5},{5,1},{9,13},{13,9},{2,6},{6,2},{1... | collective-permute-start | bytes 2015240 | tf_op jit(solution)/shard_map/ppermute | solution.py:49
  288.4 13.4 %collective-permute-start.64 = (bf16[1040,128]{1,0:T(8,128)(2,1)S(1)}, bf16[1040,128]{1,0:T(8,128)(2,1)S(1)}, u32[]{:S(2)}, u32[]{:S(2)}) collective-permute-start(bf16[1040,128]{1,0:T(8,128)(2,1)S(1)} %sum_ctx.5.refs_1_.refs_3_), channel_id=1, source_target_pairs={{0,8},{4,12},{8,0},{12,4},{1,9},{5,13},{9,1},{13,5},{2,10},{6,14},... | collective-permute-start | bytes 798728 | tf_op jit(solution)/shard_map/ppermute | solution.py:49
  288.5 22.6 %collective-permute-start.66 = (bf16[656,256]{1,0:T(8,128)(2,1)S(1)}, bf16[656,256]{1,0:T(8,128)(2,1)S(1)}, u32[]{:S(2)}, u32[]{:S(2)}) collective-permute-start(bf16[656,256]{1,0:T(8,128)(2,1)S(1)} %unite.3.refs_3_.refs_1_), channel_id=1, source_target_pairs={{0,4},{4,0},{8,12},{12,8},{1,5},{5,1},{9,13},{13,9},{2,6},{6,2},{1... | collective-permute-start | bytes 1007624 | tf_op jit(solution)/shard_map/ppermute | solution.py:49
  302.4 18.1 %collective-permute-start.65 = (bf16[1040,256]{1,0:T(8,128)(2,1)S(1)}, bf16[1040,256]{1,0:T(8,128)(2,1)S(1)}, u32[]{:S(2)}, u32[]{:S(2)}) collective-permute-start(bf16[1040,256]{1,0:T(8,128)(2,1)S(1)} %unite.5.refs_3_.refs_1_), channel_id=1, source_target_pairs={{0,4},{4,0},{8,12},{12,8},{1,5},{5,1},{9,13},{13,9},{2,6},{6,2},{1... | collective-permute-start | bytes 1597448 | tf_op jit(solution)/shard_map/ppermute | solution.py:49
  (30 other events, 209.9 us)
where the time goes:
time: 335 us; the launch traced here: 330 us
  Pallas kernels  112 us (33%)
  starting transfers between devices  96.2 us (29%)
  waiting for transfers between devices  95.6 us (29%)
  blocking collectives  14.6 us (4%)
  local copies, waits for them, and re-layouts  8.71 us (3%)
    pallas_call x44, Pallas kernels, __call__(): pl.pallas_call(run, out_shape=[jax.ShapeDtypeStruct(s, t) for s, t in out...  112 us
    ppermute x68, starting transfers between devices, swap(): return lax.ppermute(array, axis, [(i, i ^ step) for i in range(size)])  96.2 us
    ppermute x68, waiting for transfers between devices, swap(): return lax.ppermute(array, axis, [(i, i ^ step) for i in range(size)])  95.6 us
    all_gather x4, blocking collectives, both_cores(): lax.all_gather(array, 'tp', axis_index_groups=cores, axis=0, tiled=True)  9.33 us
  transfers between devices with their start and end apart: 68, of which 24 were waited for; matrix products, arithmetic and copies ran while one was open for 1% of the time, Pallas kernels for 33%

commit v1 on v0

--- a/solution.py
+++ b/solution.py
@@ -16,18 +16,18 @@
 F32 = jnp.float32
 FLOPS_PER_US = 1153e6
 SCALE = 0.764
-WEIGHTS = {"attend_back": 25.94, "attention_grad": 16.5, "feed": 3.975, "feed_grad1": 2.168, "gradient_join": 4.874, "halve": 6.466, "mix": 2.703, "norm_first_back": 0.02256, "output_join": 0.2996, "pieces": 0.09989, "project_back": 4.301, "project_sum": 0.2843, "sum_ctx": 4.169}
+WEIGHTS = {"attend_back": 25.94, "attention_grad": 16.5, "feed": 1.008, "feed_grad1": 5.67, "gradient_join": 4.874, "halve": 6.466, "mix": 2.703, "norm_first_back": 0.2153, "norm_second_back": 0.9553, "output": 0.969, "output_join": 0.1857, "pieces": 0.09989, "project_back": 4.301, "project_sum": 0.246, "sum_ctx": 4.169}
 WAIT_KEYS, WAIT_REST, WAIT_MIXING = (1,), (1,), True
 FETCH = {"keys": "mixing", "first": "feed"}
 ORDER = (
     "SB0 PC0 SB1 EX",
     "AB0 FG1 PC1 FG2",
-    "I1 AB1 BR I2",
+    "I1 AB1 I2 BR",
     "PB0 O1 PS0 PB1",
-    "FB0 AT PS1 OT",
-    "I3 O2 FB1 I4",
-    "A1 O3 OO A2",
-    "O4 JG A3 A4",
+    "FB0 OT AT I3",
+    "PS1 O2 I4 FB1",
+    "A1 O3 JG OO",
+    "A2 O4 A3 A4",
     "OJ",
 )
 CORE, ROW = 1, 2

time: 335 us -> 334 us (level)
  waiting for transfers between devices: 95.6 us -> 111 us
  Pallas kernels: 112 us -> 102 us
  starting transfers between devices: 96.2 us -> 89.8 us
    ppermute x68, waiting for transfers between devices: 95.6 us -> 111 us  [swap(): return lax.ppermute(array, axis, [(i, i ^ step) for i in range(size)])]
    pallas_call x44, Pallas kernels: 112 us -> 102 us  [__call__(): pl.pallas_call(run, out_shape=[jax.ShapeDtypeStruct(s, t) for s, t in out...]
    ppermute x68, starting transfers between devices: 96.2 us -> 89.8 us  [swap(): return lax.ppermute(array, axis, [(i, i ^ step) for i in range(size)])]
  transfers between devices with their start and end apart: 68 -> 68, of which waited for: 24 -> 23; matrix products, arithmetic and copies ran while one was open for 1% -> 1% of each run, Pallas kernels for 33% -> 30%
where the time goes in v1:
time: 334 us; the launch traced here: 329 us
  waiting for transfers between devices  111 us (33%)
  Pallas kernels  102 us (31%)
  starting transfers between devices  89.8 us (27%)
  blocking collectives  14.5 us (4%)
  local copies, waits for them, and re-layouts  8.71 us (3%)
    ppermute x68, waiting for transfers between devices, swap(): return lax.ppermute(array, axis, [(i, i ^ step) for i in range(size)])  111 us
    pallas_call x44, Pallas kernels, __call__(): pl.pallas_call(run, out_shape=[jax.ShapeDtypeStruct(s, t) for s, t in out...  102 us
    ppermute x68, starting transfers between devices, swap(): return lax.ppermute(array, axis, [(i, i ^ step) for i in range(size)])  89.8 us
    all_gather x4, blocking collectives, both_cores(): lax.all_gather(array, 'tp', axis_index_groups=cores, axis=0, tiled=True)  9.32 us
  transfers between devices with their start and end apart: 68, of which 23 were waited for; matrix products, arithmetic and copies ran while one was open for 1% of the time, Pallas kernels for 30%

profile of v1, /device:TPU:0, one launch (start us, length us, event | category | flops | bytes accessed | tf_op | source)
XLA Modules:
  0.0 329.1 jit_solution(12189256383251770040)
XLA Ops:
  2.7 2.9 collective-permute-start
  10.7 2.1 collective-permute-start.5
  12.9 3.9 %collective-permute-done.1.refs_5_.refs_9_ = bf16[512,256]{1,0:T(8,128)(2,1)S(1)} collective-permute-done((bf16[512,256]{1,0:T(8,128)(2,1)S(1)}, bf16[512,256]{1,0:T(8,128)(2,1)S(1)}, u32[]{:S(2)}, u32[]{:S(2)}) %collective-permute-start.1) | collective-permute-done | bytes 262176 | tf_op jit(solution)/shard_map/ppermute | solution.py:49
  19.8 2.6 collective-permute-start.3
  22.8 5.2 %collective-permute-done.6.refs_7_.refs_11_ = bf16[512,256]{1,0:T(8,128)(2,1)S(1)} collective-permute-done((bf16[512,256]{1,0:T(8,128)(2,1)S(1)}, bf16[512,256]{1,0:T(8,128)(2,1)S(1)}, u32[]{:S(2)}, u32[]{:S(2)}) %collective-permute-start.6) | collective-permute-done | bytes 262176 | tf_op jit(solution)/shard_map/ppermute | solution.py:49
  31.0 2.6 collective-permute-start.8
  36.3 2.6 collective-permute-start.14
  38.8 4.0 %collective-permute-start.15 = (bf16[128,512]{1,0:T(8,128)(2,1)S(1)}, bf16[128,512]{1,0:T(8,128)(2,1)S(1)}, u32[]{:S(2)}, u32[]{:S(2)}) collective-permute-start(bf16[128,512]{1,0:T(8,128)(2,1)S(1)} %get-tuple-element.127), channel_id=1, source_target_pairs={{0,8},{4,12},{8,0},{12,4},{1,9},{5,13},{9,1},{13,5},{2,10},{6,14},... | collective-permute-start | bytes 393224 | tf_op jit(solution)/shard_map/ppermute | solution.py:49
  44.5 2.0 collective-permute-start.16
  46.5 8.8 %attend.2 = (bf16[64,512]{1,0:T(8,128)(2,1)S(1)}, bf16[64,512]{1,0:T(8,128)(2,1)S(1)}, bf16[64,512]{1,0:T(8,128)(2,1)S(1)}, bf16[64,512]{1,0:T(8,128)(2,1)S(1)},...) custom-call(s32[5]{0:T(128)S(1)} %stack.47.refs_0_, s32[2]{0:T(128)S(1)} %copy-done.6, ...), custom_call_target="tpu_custom_call" | custom-call | flops 8808920064 | tf_op jit(solution)/shard_map/attend/pallas_call | solution.py:83
  55.3 3.1 collective-permute-start.11
  60.8 14.3 %attend.3 = (bf16[64,512]{1,0:T(8,128)(2,1)S(1)}, bf16[64,512]{1,0:T(8,128)(2,1)S(1)}, bf16[64,512]{1,0:T(8,128)(2,1)S(1)}, bf16[64,512]{1,0:T(8,128)(2,1)S(1)},...) custom-call(s32[5]{0:T(128)S(1)} %stack.47.refs_0_, s32[2]{0:T(128)S(1)} %copy-done.6, ...), custom_call_target="tpu_custom_call" | custom-call | flops 8808920064 | tf_op jit(solution)/shard_map/attend/pallas_call | solution.py:83
  76.3 2.2 all_gather.18.refs_1_.refs_8_
  86.0 3.4 %collective-permute-done.24.refs_3_ = bf16[64,512]{1,0:T(8,128)(2,1)S(1)} collective-permute-done((bf16[64,512]{1,0:T(8,128)(2,1)S(1)}, bf16[64,512]{1,0:T(8,128)(2,1)S(1)}, u32[]{:S(2)}, u32[]{:S(2)}) %collective-permute-start.24) | collective-permute-done | bytes 65568 | tf_op jit(solution)/shard_map/ppermute | solution.py:49
  90.0 2.2 all_gather.19.refs_1_.refs_9_
  94.8 4.4 %collective-permute-done.19.refs_2_ = bf16[256,1024]{1,0:T(8,128)(2,1)S(1)} collective-permute-done((bf16[256,1024]{1,0:T(8,128)(2,1)S(1)}, bf16[256,1024]{1,0:T(8,128)(2,1)S(1)}, u32[]{:S(2)}, u32[]{:S(2)}) %collective-permute-start.19) | collective-permute-done | bytes 524320 | tf_op jit(solution)/shard_map/ppermute | solution.py:49
  99.1 6.6 %feed.2 = (f32[256,1024]{1,0:T(8,128)S(1)}, bf16[256,1024]{1,0:T(8,128)(2,1)S(1)}, bf16[256,1024]{1,0:T(8,128)(2,1)S(1)}, bf16[256,3328]{1,0:T(8,128)(2,1)S(1)}, bf16[256,3328]{1,0:T(8,128)(2,1)S(1)}) custom-call(s32[5]{0:T(128)S(1)} %stack.47.refs_0_, bf16[256,1024]{1,0:T(8,128)(2,1)S(1)} %mix.2.refs_5_.refs_1_, ...), custom_call_target="tpu_custom_call" | custom-call | flops 887939136 | tf_op jit(solution)/shard_map/feed/pallas_call | solution.py:83
  107.3 3.0 collective-permute-done.26.refs_2_
  110.3 6.6 %feed.3 = (f32[256,1024]{1,0:T(8,128)S(1)}, bf16[256,1024]{1,0:T(8,128)(2,1)S(1)}, bf16[256,1024]{1,0:T(8,128)(2,1)S(1)}, bf16[256,3328]{1,0:T(8,128)(2,1)S(1)}, bf16[256,3328]{1,0:T(8,128)(2,1)S(1)}) custom-call(s32[5]{0:T(128)S(1)} %stack.47.refs_0_, bf16[256,1024]{1,0:T(8,128)(2,1)S(1)} %mix.3.refs_10_.refs_1_, ...), custom_call_target="tpu_custom_call" | custom-call | flops 887939136 | tf_op jit(solution)/shard_map/feed/pallas_call | solution.py:83
  118.5 3.1 collective-permute-done.27.refs_2_
  123.6 2.4 all_gather.20.refs_1_
  126.6 3.0 collective-permute-start.29
  135.7 12.7 %attend_back.2 = (bf16[192,512]{1,0:T(8,128)(2,1)S(1)}, bf16[192,512]{1,0:T(8,128)(2,1)S(1)}, bf16[192,512]{1,0:T(8,128)(2,1)S(1)}, bf16[192,512]{1,0:T(8,128)(2,1)S(1)}) custom-call(s32[5]{0:T(128)S(1)} %stack.47.refs_0_, s32[2]{0:T(128)S(1)} %copy-done.6, bf16[64,1024]{1,0:T(8,128)(2,1)S(1)} %get-tuple-element.110.refs_9_.refs_2_, ...), custom_call_target="tpu_custom_call" | custom-call | flops 22850338816 | tf_op jit(solution)/shard_map/attend_back/pallas_call | solution.py:83
  148.4 2.1 feed_grad1.1
  150.6 5.9 %collective-permute-start.37 = (bf16[656,512]{1,0:T(8,128)(2,1)S(1)}, bf16[656,512]{1,0:T(8,128)(2,1)S(1)}, u32[]{:S(2)}, u32[]{:S(2)}) collective-permute-start(bf16[656,512]{1,0:T(8,128)(2,1)S(1)} %get-tuple-element.165), channel_id=1, source_target_pairs={{0,16},{16,0},{1,17},{17,1},{2,18},{18,2},{3,19},{19,3},{4,20},{20... | collective-permute-start | bytes 2015240 | tf_op jit(solution)/shard_map/ppermute | solution.py:49
  156.4 2.6 all_gather.21.refs_1_
  164.6 3.5 %feed_grad2.1 = (f32[1312,512]{1,0:T(8,128)S(1)}, bf16[1312,512]{1,0:T(8,128)(2,1)S(1)}) custom-call(s32[5]{0:T(128)S(1)} %stack.47.refs_0_, bf16[256,3328]{1,0:T(8,128)(2,1)S(1)} %get-tuple-element.158.refs_1_, bf16[256,3328]{1,0:T(8,128)(2,1)S(1)} %collective-permute-done.35.refs_2_, bf16[256,3328]{1,0:T(8,128)(2,1)S(1)} %get-tuple-element.161.refs_3_, ...), custom_call_target="tpu_custom_call" | custom-call | flops 2995032832 | tf_op jit(solution)/shard_map/feed_grad2/pallas_call | solution.py:83
  168.1 2.1 collective-permute-done.37.refs_2_
  172.6 2.1 collective-permute-start.34
  174.8 6.8 %collective-permute-done.40.refs_12_ = bf16[64,512]{1,0:T(8,128)(2,1)S(1)} collective-permute-done((bf16[64,512]{1,0:T(8,128)(2,1)S(1)}, bf16[64,512]{1,0:T(8,128)(2,1)S(1)}, u32[]{:S(2)}, u32[]{:S(2)}) %collective-permute-start.40) | collective-permute-done | bytes 65568 | tf_op jit(solution)/shard_map/ppermute | solution.py:49
  183.5 7.6 %attend_back.3 = (bf16[192,512]{1,0:T(8,128)(2,1)S(1)}, bf16[192,512]{1,0:T(8,128)(2,1)S(1)}, bf16[192,512]{1,0:T(8,128)(2,1)S(1)}, bf16[192,512]{1,0:T(8,128)(2,1)S(1)}) custom-call(s32[5]{0:T(128)S(1)} %stack.47.refs_0_, s32[2]{0:T(128)S(1)} %copy-done.6, bf16[64,1024]{1,0:T(8,128)(2,1)S(1)} %get-tuple-element.110.refs_9_.refs_2_, ...), custom_call_target="tpu_custom_call" | custom-call | flops 22850338816 | tf_op jit(solution)/shard_map/attend_back/pallas_call | solution.py:83
  191.9 2.2 collective-permute-start.46
  194.1 2.2 collective-permute-start.47
  198.4 6.3 %collective-permute-done.43.refs_2_ = bf16[1312,512]{1,0:T(8,128)(2,1)S(1)} collective-permute-done((bf16[1312,512]{1,0:T(8,128)(2,1)S(1)}, bf16[1312,512]{1,0:T(8,128)(2,1)S(1)}, u32[]{:S(2)}, u32[]{:S(2)}) %collective-permute-start.43) | collective-permute-done | bytes 1343520 | tf_op jit(solution)/shard_map/ppermute | solution.py:49
  212.3 2.5 collective-permute-done.44.refs_2_
  216.2 2.9 attention_grad.1
  219.1 5.1 %collective-permute-start.59 = (bf16[1040,512]{1,0:T(8,128)(2,1)S(1)}, bf16[1040,512]{1,0:T(8,128)(2,1)S(1)}, u32[]{:S(2)}, u32[]{:S(2)}) collective-permute-start(bf16[1040,512]{1,0:T(8,128)(2,1)S(1)} %get-tuple-element.202), channel_id=1, source_target_pairs={{0,16},{16,0},{1,17},{17,1},{2,18},{18,2},{3,19},{19,3},{4,20},{20... | collective-permute-start | bytes 3194888 | tf_op jit(solution)/shard_map/ppermute | solution.py:49
  230.5 13.0 %collective-permute-done.55.refs_2_ = bf16[656,128]{1,0:T(8,128)(2,1)S(1)} collective-permute-done((bf16[656,128]{1,0:T(8,128)(2,1)S(1)}, bf16[656,128]{1,0:T(8,128)(2,1)S(1)}, u32[]{:S(2)}, u32[]{:S(2)}) %collective-permute-start.55) | collective-permute-done | bytes 167968 | tf_op jit(solution)/shard_map/ppermute | solution.py:49
  253.6 14.4 %collective-permute-done.48.refs_5_ = bf16[2,256,1024]{2,1,0:T(8,128)(2,1)S(1)} collective-permute-done((bf16[2,256,1024]{2,1,0:T(8,128)(2,1)S(1)}, bf16[2,256,1024]{2,1,0:T(8,128)(2,1)S(1)}, u32[]{:S(2)}, u32[]{:S(2)}) %collective-permute-start.48) | collective-permute-done | bytes 1048608 | tf_op jit(solution)/shard_map/ppermute | solution.py:49
  272.0 2.0 collective-permute-start.67
  274.0 10.3 %collective-permute-done.62.refs_1_ = bf16[1040,128]{1,0:T(8,128)(2,1)S(1)} collective-permute-done((bf16[1040,128]{1,0:T(8,128)(2,1)S(1)}, bf16[1040,128]{1,0:T(8,128)(2,1)S(1)}, u32[]{:S(2)}, u32[]{:S(2)}) %collective-permute-start.62) | collective-permute-done | bytes 266272 | tf_op jit(solution)/shard_map/ppermute | solution.py:49
  284.4 2.8 collective-permute-start.66
  287.2 11.8 %collective-permute-done.64.refs_2_ = bf16[1040,128]{1,0:T(8,128)(2,1)S(1)} collective-permute-done((bf16[1040,128]{1,0:T(8,128)(2,1)S(1)}, bf16[1040,128]{1,0:T(8,128)(2,1)S(1)}, u32[]{:S(2)}, u32[]{:S(2)}) %collective-permute-start.64) | collective-permute-done | bytes 266272 | tf_op jit(solution)/shard_map/ppermute | solution.py:49
  302.9 5.6 %collective-permute-done.66.refs_2_ = bf16[656,256]{1,0:T(8,128)(2,1)S(1)} collective-permute-done((bf16[656,256]{1,0:T(8,128)(2,1)S(1)}, bf16[656,256]{1,0:T(8,128)(2,1)S(1)}, u32[]{:S(2)}, u32[]{:S(2)}) %collective-permute-start.66) | collective-permute-done | bytes 335904 | tf_op jit(solution)/shard_map/ppermute | solution.py:49
  310.1 2.7 feed_end.1
  312.9 6.8 %collective-permute-done.65.refs_2_ = bf16[1040,256]{1,0:T(8,128)(2,1)S(1)} collective-permute-done((bf16[1040,256]{1,0:T(8,128)(2,1)S(1)}, bf16[1040,256]{1,0:T(8,128)(2,1)S(1)}, u32[]{:S(2)}, u32[]{:S(2)}) %collective-permute-start.65) | collective-permute-done | bytes 532512 | tf_op jit(solution)/shard_map/ppermute | solution.py:49
  321.0 2.1 attention_end.1
  323.1 5.2 %all-gather.1 = f32[4,2,512]{2,1,0:T(2,128)S(1)} all-gather(f32[1,2,512]{2,1,0:T(2,128)S(1)} %bitcast.28), channel_id=2, replica_groups=mesh['fsdp'=2,'ctx'=4,'tp'=4] {'tp'}, dimensions={0}, use_global_device_ids=true | all-gather | bytes 20480 | tf_op jit(solution)/shard_map/all_gather | solution.py:950
  (174 shorter events, 93.8 us)
Async XLA Ops:
  10.7 12.1 %collective-permute-start.5 = (bf16[512,256]{1,0:T(8,128)(2,1)S(1)}, bf16[512,256]{1,0:T(8,128)(2,1)S(1)}, u32[]{:S(2)}, u32[]{:S(2)}) collective-permute-start(bf16[512,256]{1,0:T(8,128)(2,1)S(1)} %copy-done.5), channel_id=1, source_target_pairs={{0,16},{16,0},{1,17},{17,1},{2,18},{18,2},{3,19},{19,3},{4,20},{20... | collective-permute-start | bytes 786440 | tf_op jit(solution)/shard_map/ppermute | solution.py:49
  12.8 15.2 %collective-permute-start.6 = (bf16[512,256]{1,0:T(8,128)(2,1)S(1)}, bf16[512,256]{1,0:T(8,128)(2,1)S(1)}, u32[]{:S(2)}, u32[]{:S(2)}) collective-permute-start(bf16[512,256]{1,0:T(8,128)(2,1)S(1)} %get-tuple-element.115.refs_6_.refs_10_), channel_id=1, source_target_pairs={{0,16},{16,0},{1,17},{17,1},{2,18},{18,2},{3,19},{19,3},{4,20},{20... | collective-permute-start | bytes 786440 | tf_op jit(solution)/shard_map/ppermute | solution.py:49
  19.8 13.8 %collective-permute-start.3 = (bf16[64,1024]{1,0:T(8,128)(2,1)S(1)}, bf16[64,1024]{1,0:T(8,128)(2,1)S(1)}, u32[]{:S(2)}, u32[]{:S(2)}) collective-permute-start(bf16[64,1024]{1,0:T(8,128)(2,1)S(1)} %get-tuple-element.112), channel_id=1, source_target_pairs={{0,8},{4,12},{8,0},{12,4},{1,9},{5,13},{9,1},{13,5},{2,10},{6,14},... | collective-permute-start | bytes 393224 | tf_op jit(solution)/shard_map/ppermute | solution.py:49
  22.5 11.5 %collective-permute-start.4 = (bf16[64,1024]{1,0:T(8,128)(2,1)S(1)}, bf16[64,1024]{1,0:T(8,128)(2,1)S(1)}, u32[]{:S(2)}, u32[]{:S(2)}) collective-permute-start(bf16[64,1024]{1,0:T(8,128)(2,1)S(1)} %get-tuple-element.113), channel_id=1, source_target_pairs={{0,12},{4,8},{8,4},{12,0},{1,13},{5,9},{9,5},{13,1},{2,14},{6,10},... | collective-permute-start | bytes 393224 | tf_op jit(solution)/shard_map/ppermute | solution.py:49
  22.8 11.3 %collective-permute-start.10 = (bf16[256,512]{1,0:T(8,128)(2,1)S(1)}, bf16[256,512]{1,0:T(8,128)(2,1)S(1)}, u32[]{:S(2)}, u32[]{:S(2)}) collective-permute-start(bf16[256,512]{1,0:T(8,128)(2,1)S(1)} %copy-done.4), channel_id=1, source_target_pairs={{0,16},{16,0},{1,17},{17,1},{2,18},{18,2},{3,19},{19,3},{4,20},{20... | collective-permute-start | bytes 786440 | tf_op jit(solution)/shard_map/ppermute | solution.py:49
  31.0 13.5 %collective-permute-start.8 = (bf16[128,512]{1,0:T(8,128)(2,1)S(1)}, bf16[128,512]{1,0:T(8,128)(2,1)S(1)}, u32[]{:S(2)}, u32[]{:S(2)}) collective-permute-start(bf16[128,512]{1,0:T(8,128)(2,1)S(1)} %get-tuple-element.118), channel_id=1, source_target_pairs={{0,8},{4,12},{8,0},{12,4},{1,9},{5,13},{9,1},{13,5},{2,10},{6,14},... | collective-permute-start | bytes 393224 | tf_op jit(solution)/shard_map/ppermute | solution.py:49
  33.6 12.9 %collective-permute-start.9 = (bf16[128,512]{1,0:T(8,128)(2,1)S(1)}, bf16[128,512]{1,0:T(8,128)(2,1)S(1)}, u32[]{:S(2)}, u32[]{:S(2)}) collective-permute-start(bf16[128,512]{1,0:T(8,128)(2,1)S(1)} %get-tuple-element.119), channel_id=1, source_target_pairs={{0,12},{4,8},{8,4},{12,0},{1,13},{5,9},{9,5},{13,1},{2,14},{6,10},... | collective-permute-start | bytes 393224 | tf_op jit(solution)/shard_map/ppermute | solution.py:49
  34.0 45.7 %collective-permute-start.20 = (bf16[1968,512]{1,0:T(8,128)(2,1)S(1)}, bf16[1968,512]{1,0:T(8,128)(2,1)S(1)}, u32[]{:S(2)}, u32[]{:S(2)}) collective-permute-start(bf16[1968,512]{1,0:T(8,128)(2,1)S(1)} %pad_maximum_fusion.refs_6_), channel_id=1, source_target_pairs={{0,16},{16,0},{1,17},{17,1},{2,18},{18,2},{3,19},{19,3},{4,20},{20... | collective-permute-start | bytes 6045704 | tf_op jit(solution)/shard_map/ppermute | solution.py:49
  36.3 22.1 %collective-permute-start.14 = (bf16[128,512]{1,0:T(8,128)(2,1)S(1)}, bf16[128,512]{1,0:T(8,128)(2,1)S(1)}, u32[]{:S(2)}, u32[]{:S(2)}) collective-permute-start(bf16[128,512]{1,0:T(8,128)(2,1)S(1)} %get-tuple-element.126), channel_id=1, source_target_pairs={{0,4},{4,0},{8,12},{12,8},{1,5},{5,1},{9,13},{13,9},{2,6},{6,2},{1... | collective-permute-start | bytes 393224 | tf_op jit(solution)/shard_map/ppermute | solution.py:49
  38.8 20.4 %collective-permute-start.15 = (bf16[128,512]{1,0:T(8,128)(2,1)S(1)}, bf16[128,512]{1,0:T(8,128)(2,1)S(1)}, u32[]{:S(2)}, u32[]{:S(2)}) collective-permute-start(bf16[128,512]{1,0:T(8,128)(2,1)S(1)} %get-tuple-element.127), channel_id=1, source_target_pairs={{0,8},{4,12},{8,0},{12,4},{1,9},{5,13},{9,1},{13,5},{2,10},{6,14},... | collective-permute-start | bytes 393224 | tf_op jit(solution)/shard_map/ppermute | solution.py:49
  44.5 16.3 %collective-permute-start.16 = (bf16[128,512]{1,0:T(8,128)(2,1)S(1)}, bf16[128,512]{1,0:T(8,128)(2,1)S(1)}, u32[]{:S(2)}, u32[]{:S(2)}) collective-permute-start(bf16[128,512]{1,0:T(8,128)(2,1)S(1)} %get-tuple-element.128), channel_id=1, source_target_pairs={{0,12},{4,8},{8,4},{12,0},{1,13},{5,9},{9,5},{13,1},{2,14},{6,10},... | collective-permute-start | bytes 393224 | tf_op jit(solution)/shard_map/ppermute | solution.py:49
  55.3 19.8 %collective-permute-start.11 = (bf16[64,512]{1,0:T(8,128)(2,1)S(1)}, bf16[64,512]{1,0:T(8,128)(2,1)S(1)}, u32[]{:S(2)}, u32[]{:S(2)}) collective-permute-start(bf16[64,512]{1,0:T(8,128)(2,1)S(1)} %get-tuple-element.123), channel_id=1, source_target_pairs={{0,4},{4,0},{8,12},{12,8},{1,5},{5,1},{9,13},{13,9},{2,6},{6,2},{1... | collective-permute-start | bytes 196616 | tf_op jit(solution)/shard_map/ppermute | solution.py:49
  58.4 16.7 %collective-permute-start.12 = (bf16[64,512]{1,0:T(8,128)(2,1)S(1)}, bf16[64,512]{1,0:T(8,128)(2,1)S(1)}, u32[]{:S(2)}, u32[]{:S(2)}) collective-permute-start(bf16[64,512]{1,0:T(8,128)(2,1)S(1)} %get-tuple-element.124), channel_id=1, source_target_pairs={{0,8},{4,12},{8,0},{12,4},{1,9},{5,13},{9,1},{13,5},{2,10},{6,14},... | collective-permute-start | bytes 196616 | tf_op jit(solution)/shard_map/ppermute | solution.py:49
  59.2 15.9 %collective-permute-start.13 = (bf16[64,512]{1,0:T(8,128)(2,1)S(1)}, bf16[64,512]{1,0:T(8,128)(2,1)S(1)}, u32[]{:S(2)}, u32[]{:S(2)}) collective-permute-start(bf16[64,512]{1,0:T(8,128)(2,1)S(1)} %get-tuple-element.125), channel_id=1, source_target_pairs={{0,12},{4,8},{8,4},{12,0},{1,13},{5,9},{9,5},{13,1},{2,14},{6,10},... | collective-permute-start | bytes 196616 | tf_op jit(solution)/shard_map/ppermute | solution.py:49
  79.5 19.6 %collective-permute-start.21 = (bf16[1968,512]{1,0:T(8,128)(2,1)S(1)}, bf16[1968,512]{1,0:T(8,128)(2,1)S(1)}, u32[]{:S(2)}, u32[]{:S(2)}) collective-permute-start(bf16[1968,512]{1,0:T(8,128)(2,1)S(1)} %pad_maximum_fusion.refs_6_), channel_id=1, source_target_pairs={{0,1},{1,0},{2,3},{3,2},{4,5},{5,4},{6,7},{7,6},{8,9},{9,8},{10,11... | collective-permute-start | bytes 6045704 | tf_op jit(solution)/shard_map/ppermute | solution.py:49
  79.7 19.4 %collective-permute-start.22 = (bf16[1968,512]{1,0:T(8,128)(2,1)S(1)}, bf16[1968,512]{1,0:T(8,128)(2,1)S(1)}, u32[]{:S(2)}, u32[]{:S(2)}) collective-permute-start(bf16[1968,512]{1,0:T(8,128)(2,1)S(1)} %collective-permute-done.20.refs_7_), channel_id=1, source_target_pairs={{0,1},{1,0},{2,3},{3,2},{4,5},{5,4},{6,7},{7,6},{8,9},{9,8},{10,11... | collective-permute-start | bytes 6045704 | tf_op jit(solution)/shard_map/ppermute | solution.py:49
  84.4 14.7 %collective-permute-start.19 = (bf16[256,1024]{1,0:T(8,128)(2,1)S(1)}, bf16[256,1024]{1,0:T(8,128)(2,1)S(1)}, u32[]{:S(2)}, u32[]{:S(2)}) collective-permute-start(bf16[256,1024]{1,0:T(8,128)(2,1)S(1)} %mix.2.refs_5_.refs_1_), channel_id=1, source_target_pairs={{0,2},{1,3},{2,0},{3,1},{4,6},{5,7},{6,4},{7,5},{8,10},{9,11},{10,... | collective-permute-start | bytes 1572872 | tf_op jit(solution)/shard_map/ppermute | solution.py:49
  93.2 17.2 %collective-permute-start.26 = (bf16[256,1024]{1,0:T(8,128)(2,1)S(1)}, bf16[256,1024]{1,0:T(8,128)(2,1)S(1)}, u32[]{:S(2)}, u32[]{:S(2)}) collective-permute-start(bf16[256,1024]{1,0:T(8,128)(2,1)S(1)} %mix.3.refs_10_.refs_1_), channel_id=1, source_target_pairs={{0,2},{1,3},{2,0},{3,1},{4,6},{5,7},{6,4},{7,5},{8,10},{9,11},{10,... | collective-permute-start | bytes 1572872 | tf_op jit(solution)/shard_map/ppermute | solution.py:49
  105.7 15.9 %collective-permute-start.27 = (bf16[256,1024]{1,0:T(8,128)(2,1)S(1)}, bf16[256,1024]{1,0:T(8,128)(2,1)S(1)}, u32[]{:S(2)}, u32[]{:S(2)}) collective-permute-start(bf16[256,1024]{1,0:T(8,128)(2,1)S(1)} %get-tuple-element.144.refs_1_), channel_id=1, source_target_pairs={{0,2},{1,3},{2,0},{3,1},{4,6},{5,7},{6,4},{7,5},{8,10},{9,11},{10,... | collective-permute-start | bytes 1572872 | tf_op jit(solution)/shard_map/ppermute | solution.py:49
  116.9 14.3 %collective-permute-start.31 = (bf16[256,1024]{1,0:T(8,128)(2,1)S(1)}, bf16[256,1024]{1,0:T(8,128)(2,1)S(1)}, u32[]{:S(2)}, u32[]{:S(2)}) collective-permute-start(bf16[256,1024]{1,0:T(8,128)(2,1)S(1)} %get-tuple-element.152.refs_1_), channel_id=1, source_target_pairs={{0,2},{1,3},{2,0},{3,1},{4,6},{5,7},{6,4},{7,5},{8,10},{9,11},{10,... | collective-permute-start | bytes 1572872 | tf_op jit(solution)/shard_map/ppermute | solution.py:49
  133.3 15.2 %collective-permute-start.35 = (bf16[256,3328]{1,0:T(8,128)(2,1)S(1)}, bf16[256,3328]{1,0:T(8,128)(2,1)S(1)}, u32[]{:S(2)}, u32[]{:S(2)}) collective-permute-start(bf16[256,3328]{1,0:T(8,128)(2,1)S(1)} %get-tuple-element.160), channel_id=1, source_target_pairs={{0,1},{1,0},{2,3},{3,2},{4,5},{5,4},{6,7},{7,6},{8,9},{9,8},{10,11... | collective-permute-start | bytes 5111816 | tf_op jit(solution)/shard_map/ppermute | solution.py:49
  133.3 15.1 %collective-permute-start.36 = (bf16[256,3328]{1,0:T(8,128)(2,1)S(1)}, bf16[256,3328]{1,0:T(8,128)(2,1)S(1)}, u32[]{:S(2)}, u32[]{:S(2)}) collective-permute-start(bf16[256,3328]{1,0:T(8,128)(2,1)S(1)} %get-tuple-element.163), channel_id=1, source_target_pairs={{0,1},{1,0},{2,3},{3,2},{4,5},{5,4},{6,7},{7,6},{8,9},{9,8},{10,11... | collective-permute-start | bytes 5111816 | tf_op jit(solution)/shard_map/ppermute | solution.py:49
  150.6 19.6 %collective-permute-start.37 = (bf16[656,512]{1,0:T(8,128)(2,1)S(1)}, bf16[656,512]{1,0:T(8,128)(2,1)S(1)}, u32[]{:S(2)}, u32[]{:S(2)}) collective-permute-start(bf16[656,512]{1,0:T(8,128)(2,1)S(1)} %get-tuple-element.165), channel_id=1, source_target_pairs={{0,16},{16,0},{1,17},{17,1},{2,18},{18,2},{3,19},{19,3},{4,20},{20... | collective-permute-start | bytes 2015240 | tf_op jit(solution)/shard_map/ppermute | solution.py:49
  159.0 32.9 %collective-permute-start.32 = (bf16[192,512]{1,0:T(8,128)(2,1)S(1)}, bf16[192,512]{1,0:T(8,128)(2,1)S(1)}, u32[]{:S(2)}, u32[]{:S(2)}) collective-permute-start(bf16[192,512]{1,0:T(8,128)(2,1)S(1)} %get-tuple-element.155), channel_id=1, source_target_pairs={{0,4},{4,0},{8,12},{12,8},{1,5},{5,1},{9,13},{13,9},{2,6},{6,2},{1... | collective-permute-start | bytes 589832 | tf_op jit(solution)/shard_map/ppermute | solution.py:49
  160.2 33.8 %collective-permute-start.33 = (bf16[192,512]{1,0:T(8,128)(2,1)S(1)}, bf16[192,512]{1,0:T(8,128)(2,1)S(1)}, u32[]{:S(2)}, u32[]{:S(2)}) collective-permute-start(bf16[192,512]{1,0:T(8,128)(2,1)S(1)} %get-tuple-element.156), channel_id=1, source_target_pairs={{0,8},{4,12},{8,0},{12,4},{1,9},{5,13},{9,1},{13,5},{2,10},{6,14},... | collective-permute-start | bytes 589832 | tf_op jit(solution)/shard_map/ppermute | solution.py:49
  163.0 18.5 %collective-permute-start.40 = (bf16[64,512]{1,0:T(8,128)(2,1)S(1)}, bf16[64,512]{1,0:T(8,128)(2,1)S(1)}, u32[]{:S(2)}, u32[]{:S(2)}) collective-permute-start(bf16[64,512]{1,0:T(8,128)(2,1)S(1)} %get-tuple-element.172), channel_id=1, source_target_pairs={{0,8},{4,12},{8,0},{12,4},{1,9},{5,13},{9,1},{13,5},{2,10},{6,14},... | collective-permute-start | bytes 196616 | tf_op jit(solution)/shard_map/ppermute | solution.py:49
  170.2 11.4 %collective-permute-start.41 = (bf16[64,512]{1,0:T(8,128)(2,1)S(1)}, bf16[64,512]{1,0:T(8,128)(2,1)S(1)}, u32[]{:S(2)}, u32[]{:S(2)}) collective-permute-start(bf16[64,512]{1,0:T(8,128)(2,1)S(1)} %get-tuple-element.173), channel_id=1, source_target_pairs={{0,12},{4,8},{8,4},{12,0},{1,13},{5,9},{9,5},{13,1},{2,14},{6,10},... | collective-permute-start | bytes 196616 | tf_op jit(solution)/shard_map/ppermute | solution.py:49
  172.6 23.7 %collective-permute-start.34 = (bf16[192,512]{1,0:T(8,128)(2,1)S(1)}, bf16[192,512]{1,0:T(8,128)(2,1)S(1)}, u32[]{:S(2)}, u32[]{:S(2)}) collective-permute-start(bf16[192,512]{1,0:T(8,128)(2,1)S(1)} %get-tuple-element.157), channel_id=1, source_target_pairs={{0,12},{4,8},{8,4},{12,0},{1,13},{5,9},{9,5},{13,1},{2,14},{6,10},... | collective-permute-start | bytes 589832 | tf_op jit(solution)/shard_map/ppermute | solution.py:49
  181.6 23.1 %collective-permute-start.43 = (bf16[1312,512]{1,0:T(8,128)(2,1)S(1)}, bf16[1312,512]{1,0:T(8,128)(2,1)S(1)}, u32[]{:S(2)}, u32[]{:S(2)}) collective-permute-start(bf16[1312,512]{1,0:T(8,128)(2,1)S(1)} %get-tuple-element.179), channel_id=1, source_target_pairs={{0,16},{16,0},{1,17},{17,1},{2,18},{18,2},{3,19},{19,3},{4,20},{20... | collective-permute-start | bytes 4030472 | tf_op jit(solution)/shard_map/ppermute | solution.py:49
  191.1 16.0 %collective-permute-start.45 = (bf16[192,512]{1,0:T(8,128)(2,1)S(1)}, bf16[192,512]{1,0:T(8,128)(2,1)S(1)}, u32[]{:S(2)}, u32[]{:S(2)}) collective-permute-start(bf16[192,512]{1,0:T(8,128)(2,1)S(1)} %get-tuple-element.183), channel_id=1, source_target_pairs={{0,4},{4,0},{8,12},{12,8},{1,5},{5,1},{9,13},{13,9},{2,6},{6,2},{1... | collective-permute-start | bytes 589832 | tf_op jit(solution)/shard_map/ppermute | solution.py:49
  191.9 15.7 %collective-permute-start.46 = (bf16[192,512]{1,0:T(8,128)(2,1)S(1)}, bf16[192,512]{1,0:T(8,128)(2,1)S(1)}, u32[]{:S(2)}, u32[]{:S(2)}) collective-permute-start(bf16[192,512]{1,0:T(8,128)(2,1)S(1)} %get-tuple-element.184), channel_id=1, source_target_pairs={{0,8},{4,12},{8,0},{12,4},{1,9},{5,13},{9,1},{13,5},{2,10},{6,14},... | collective-permute-start | bytes 589832 | tf_op jit(solution)/shard_map/ppermute | solution.py:49
  194.1 14.5 %collective-permute-start.47 = (bf16[192,512]{1,0:T(8,128)(2,1)S(1)}, bf16[192,512]{1,0:T(8,128)(2,1)S(1)}, u32[]{:S(2)}, u32[]{:S(2)}) collective-permute-start(bf16[192,512]{1,0:T(8,128)(2,1)S(1)} %get-tuple-element.185), channel_id=1, source_target_pairs={{0,12},{4,8},{8,4},{12,0},{1,13},{5,9},{9,5},{13,1},{2,14},{6,10},... | collective-permute-start | bytes 589832 | tf_op jit(solution)/shard_map/ppermute | solution.py:49
  207.7 17.0 %collective-permute-start.51 = (bf16[656,128]{1,0:T(8,128)(2,1)S(1)}, bf16[656,128]{1,0:T(8,128)(2,1)S(1)}, u32[]{:S(2)}, u32[]{:S(2)}) collective-permute-start(bf16[656,128]{1,0:T(8,128)(2,1)S(1)} %get-tuple-element.190), channel_id=1, source_target_pairs={{0,8},{4,12},{8,0},{12,4},{1,9},{5,13},{9,1},{13,5},{2,10},{6,14},... | collective-permute-start | bytes 503816 | tf_op jit(solution)/shard_map/ppermute | solution.py:49
  208.6 21.0 %collective-permute-start.56 = (bf16[1312,256]{1,0:T(8,128)(2,1)S(1)}, bf16[1312,256]{1,0:T(8,128)(2,1)S(1)}, u32[]{:S(2)}, u32[]{:S(2)}) collective-permute-start(bf16[1312,256]{1,0:T(8,128)(2,1)S(1)} %get-tuple-element.199), channel_id=1, source_target_pairs={{0,4},{4,0},{8,12},{12,8},{1,5},{5,1},{9,13},{13,9},{2,6},{6,2},{1... | collective-permute-start | bytes 2015240 | tf_op jit(solution)/shard_map/ppermute | solution.py:49
  219.1 29.3 %collective-permute-start.59 = (bf16[1040,512]{1,0:T(8,128)(2,1)S(1)}, bf16[1040,512]{1,0:T(8,128)(2,1)S(1)}, u32[]{:S(2)}, u32[]{:S(2)}) collective-permute-start(bf16[1040,512]{1,0:T(8,128)(2,1)S(1)} %get-tuple-element.202), channel_id=1, source_target_pairs={{0,16},{16,0},{1,17},{17,1},{2,18},{18,2},{3,19},{19,3},{4,20},{20... | collective-permute-start | bytes 3194888 | tf_op jit(solution)/shard_map/ppermute | solution.py:49
  224.3 27.2 %collective-permute-start.49 = (bf16[256,1024]{1,0:T(8,128)(2,1)S(1)}, bf16[256,1024]{1,0:T(8,128)(2,1)S(1)}, u32[]{:S(2)}, u32[]{:S(2)}) collective-permute-start(bf16[256,1024]{1,0:T(8,128)(2,1)S(1)} %norm_first_back.2.refs_14_.refs_1_), channel_id=1, source_target_pairs={{0,1},{1,0},{2,3},{3,2},{4,5},{5,4},{6,7},{7,6},{8,9},{9,8},{10,11... | collective-permute-start | bytes 1572872 | tf_op jit(solution)/shard_map/ppermute | solution.py:49
  224.7 18.8 %collective-permute-start.55 = (bf16[656,128]{1,0:T(8,128)(2,1)S(1)}, bf16[656,128]{1,0:T(8,128)(2,1)S(1)}, u32[]{:S(2)}, u32[]{:S(2)}) collective-permute-start(bf16[656,128]{1,0:T(8,128)(2,1)S(1)} %sum_ctx.3.refs_2_.refs_1_), channel_id=1, source_target_pairs={{0,8},{4,12},{8,0},{12,4},{1,9},{5,13},{9,1},{13,5},{2,10},{6,14},... | collective-permute-start | bytes 503816 | tf_op jit(solution)/shard_map/ppermute | solution.py:49
  226.1 19.5 %collective-permute-start.54 = (bf16[256,1024]{1,0:T(8,128)(2,1)S(1)}, bf16[256,1024]{1,0:T(8,128)(2,1)S(1)}, u32[]{:S(2)}, u32[]{:S(2)}) collective-permute-start(bf16[256,1024]{1,0:T(8,128)(2,1)S(1)} %project_sum.3.refs_3_.refs_1_), channel_id=1, source_target_pairs={{0,2},{1,3},{2,0},{3,1},{4,6},{5,7},{6,4},{7,5},{8,10},{9,11},{10,... | collective-permute-start | bytes 1572872 | tf_op jit(solution)/shard_map/ppermute | solution.py:49
  230.3 20.1 %collective-permute-start.58 = (bf16[1312,128]{1,0:T(8,128)(2,1)S(1)}, bf16[1312,128]{1,0:T(8,128)(2,1)S(1)}, u32[]{:S(2)}, u32[]{:S(2)}) collective-permute-start(bf16[1312,128]{1,0:T(8,128)(2,1)S(1)} %get-tuple-element.201), channel_id=1, source_target_pairs={{0,8},{4,12},{8,0},{12,4},{1,9},{5,13},{9,1},{13,5},{2,10},{6,14},... | collective-permute-start | bytes 1007624 | tf_op jit(solution)/shard_map/ppermute | solution.py:49
  243.5 24.5 %collective-permute-start.48 = (bf16[2,256,1024]{2,1,0:T(8,128)(2,1)S(1)}, bf16[2,256,1024]{2,1,0:T(8,128)(2,1)S(1)}, u32[]{:S(2)}, u32[]{:S(2)}) collective-permute-start(bf16[2,256,1024]{2,1,0:T(8,128)(2,1)S(1)} %pad_maximum_fusion.1), channel_id=1, source_target_pairs={{0,2},{1,3},{2,0},{3,1},{4,6},{5,7},{6,4},{7,5},{8,10},{9,11},{10,... | collective-permute-start | bytes 3145736 | tf_op jit(solution)/shard_map/ppermute | solution.py:49
  249.2 21.2 %collective-permute-start.61 = (bf16[1040,256]{1,0:T(8,128)(2,1)S(1)}, bf16[1040,256]{1,0:T(8,128)(2,1)S(1)}, u32[]{:S(2)}, u32[]{:S(2)}) collective-permute-start(bf16[1040,256]{1,0:T(8,128)(2,1)S(1)} %get-tuple-element.204), channel_id=1, source_target_pairs={{0,4},{4,0},{8,12},{12,8},{1,5},{5,1},{9,13},{13,9},{2,6},{6,2},{1... | collective-permute-start | bytes 1597448 | tf_op jit(solution)/shard_map/ppermute | solution.py:49
  250.4 20.9 %collective-permute-start.63 = (bf16[1312,128]{1,0:T(8,128)(2,1)S(1)}, bf16[1312,128]{1,0:T(8,128)(2,1)S(1)}, u32[]{:S(2)}, u32[]{:S(2)}) collective-permute-start(bf16[1312,128]{1,0:T(8,128)(2,1)S(1)} %sum_ctx.4.refs_5_.refs_1_), channel_id=1, source_target_pairs={{0,8},{4,12},{8,0},{12,4},{1,9},{5,13},{9,1},{13,5},{2,10},{6,14},... | collective-permute-start | bytes 1007624 | tf_op jit(solution)/shard_map/ppermute | solution.py:49
  271.2 13.1 %collective-permute-start.62 = (bf16[1040,128]{1,0:T(8,128)(2,1)S(1)}, bf16[1040,128]{1,0:T(8,128)(2,1)S(1)}, u32[]{:S(2)}, u32[]{:S(2)}) collective-permute-start(bf16[1040,128]{1,0:T(8,128)(2,1)S(1)} %get-tuple-element.206), channel_id=1, source_target_pairs={{0,8},{4,12},{8,0},{12,4},{1,9},{5,13},{9,1},{13,5},{2,10},{6,14},... | collective-permute-start | bytes 798728 | tf_op jit(solution)/shard_map/ppermute | solution.py:49
  271.2 29.7 %collective-permute-start.60 = (bf16[2,256,1024]{2,1,0:T(8,128)(2,1)S(1)}, bf16[2,256,1024]{2,1,0:T(8,128)(2,1)S(1)}, u32[]{:S(2)}, u32[]{:S(2)}) collective-permute-start(bf16[2,256,1024]{2,1,0:T(8,128)(2,1)S(1)} %output.1.refs_3_.refs_1_), channel_id=1, source_target_pairs={{0,1},{1,0},{2,3},{3,2},{4,5},{5,4},{6,7},{7,6},{8,9},{9,8},{10,11... | collective-permute-start | bytes 3145736 | tf_op jit(solution)/shard_map/ppermute | solution.py:49
  272.0 36.5 %collective-permute-start.67 = (bf16[1312,256]{1,0:T(8,128)(2,1)S(1)}, bf16[1312,256]{1,0:T(8,128)(2,1)S(1)}, u32[]{:S(2)}, u32[]{:S(2)}) collective-permute-start(bf16[1312,256]{1,0:T(8,128)(2,1)S(1)} %unite.4.refs_2_.refs_3_), channel_id=1, source_target_pairs={{0,4},{4,0},{8,12},{12,8},{1,5},{5,1},{9,13},{13,9},{2,6},{6,2},{1... | collective-permute-start | bytes 2015240 | tf_op jit(solution)/shard_map/ppermute | solution.py:49
  284.3 14.6 %collective-permute-start.64 = (bf16[1040,128]{1,0:T(8,128)(2,1)S(1)}, bf16[1040,128]{1,0:T(8,128)(2,1)S(1)}, u32[]{:S(2)}, u32[]{:S(2)}) collective-permute-start(bf16[1040,128]{1,0:T(8,128)(2,1)S(1)} %sum_ctx.5.refs_1_.refs_3_), channel_id=1, source_target_pairs={{0,8},{4,12},{8,0},{12,4},{1,9},{5,13},{9,1},{13,5},{2,10},{6,14},... | collective-permute-start | bytes 798728 | tf_op jit(solution)/shard_map/ppermute | solution.py:49
  284.4 24.1 %collective-permute-start.66 = (bf16[656,256]{1,0:T(8,128)(2,1)S(1)}, bf16[656,256]{1,0:T(8,128)(2,1)S(1)}, u32[]{:S(2)}, u32[]{:S(2)}) collective-permute-start(bf16[656,256]{1,0:T(8,128)(2,1)S(1)} %unite.3.refs_6_.refs_1_), channel_id=1, source_target_pairs={{0,4},{4,0},{8,12},{12,8},{1,5},{5,1},{9,13},{13,9},{2,6},{6,2},{1... | collective-permute-start | bytes 1007624 | tf_op jit(solution)/shard_map/ppermute | solution.py:49
  299.6 20.1 %collective-permute-start.65 = (bf16[1040,256]{1,0:T(8,128)(2,1)S(1)}, bf16[1040,256]{1,0:T(8,128)(2,1)S(1)}, u32[]{:S(2)}, u32[]{:S(2)}) collective-permute-start(bf16[1040,256]{1,0:T(8,128)(2,1)S(1)} %unite.5.refs_3_.refs_1_), channel_id=1, source_target_pairs={{0,4},{4,0},{8,12},{12,8},{1,5},{5,1},{9,13},{13,9},{2,6},{6,2},{1... | collective-permute-start | bytes 1597448 | tf_op jit(solution)/shard_map/ppermute | solution.py:49
  (30 other events, 202.6 us)
